TPU v7x, 256 devices: a whole 4x4x8 slice. The times are simulated.
256 devices in a mesh: strike: 32 (over x_lo, z, core), depth: 8 (over x_hi, y).
Axes of the slice: x: 4 (x_hi: 2, x_lo: 2; x = x_hi * 2 + x_lo), y: 4, z: 8, core: 2. Of those that a mesh axis runs over, the one named last changes fastest.
Arguments:
- sliding_speed: float32 [768, 8192], P('depth', 'strike'), may hold values from 0.1 to 10
- offset_displacement: float32 [768, 8192], P('depth', 'strike'), may hold values from -6 to 6
- contact_memory: float32 [768, 8192], P('depth', 'strike'), may hold values from -1 to 1
- clamping_traction: float32 [768, 8192], P('depth', 'strike'), may hold values from 5 to 9
- instant_effect_a: float32 [768, 8192], P('depth', 'strike'), may hold values from 0.5 to 1
- healing_effect_b: float32 [768, 8192], P('depth', 'strike'), may hold values from 0.5 to 1.5
- ambient_traction: float32 [768, 8192], P('depth', 'strike'), may hold values from 0 to 10
- heat_level: float32 [32, 768, 8192], P(None, 'depth', 'strike'), may hold values from -4 to 4
- fluid_load: float32 [32, 768, 8192], P(None, 'depth', 'strike'), may hold values from -4 to 4
Outputs:
- sliding_acceleration: float32 [768, 8192], P('depth', 'strike')
- memory_change: float32 [768, 8192], P('depth', 'strike')
- heat_level_change: float32 [32, 768, 8192], P(None, 'depth', 'strike')
- fluid_load_change: float32 [32, 768, 8192], P(None, 'depth', 'strike')
All inputs are finite; a program needn't handle non-finite values.
Results may differ from a plain program's by a relative error of at most 0.00005.
Values sent between devices are 32-bit elements; how exact they have to be, the bound alone decides.
No kernel may reach another device: no remote copies, remote signals or barrier semaphores. Data moves between devices by JAX's collectives and lax.ppermute only.
A program may use at most 128 MiB of HBM per device.

v0:
```python
import math

import jax
import jax.numpy as jnp
from jax import lax
from jax.sharding import PartitionSpec as P

HEAT_GAIN = 0.05
HEAT_DIFFUSIVITY = 0.3
FLUID_DIFFUSIVITY = 0.45
FLUID_TOGGLE = 0.6
REF_FRICTION = 0.5
DAMPING = 0.5
RELAXATION = 0.2
ELASTIC = 4.0 / 3.0
HEAT_WIDTH = 4.0
HIGHEST = lax.Precision.HIGHEST


def discrete_laplacian(values_in):
    above_part = jnp.concatenate([values_in[1:], jnp.zeros_like(values_in[:1])], 0)
    below_part = jnp.concatenate([values_in[1:2], values_in[:-1]], 0)
    return above_part - 2.0 * values_in + below_part


def interface_tendencies(
    sliding_speed,
    contact_memory,
    clamping_traction,
    instant_effect_a,
    healing_effect_b,
    heat_level,
    fluid_load,
):
    argument = 0.5 * sliding_speed * jnp.exp(contact_memory / instant_effect_a)
    friction = instant_effect_a * jnp.log(argument + jnp.sqrt(argument * argument + 1.0))
    root_term = jnp.sqrt(
        4.0 * jnp.exp(-2.0 * contact_memory / instant_effect_a) + sliding_speed * sliding_speed
    )
    effective = clamping_traction - fluid_load[0]
    sliding_traction = effective * friction
    across_sample_count = jnp.arange(heat_level.shape[0]).astype(jnp.float32)
    across_layout = jnp.exp(-((across_sample_count / HEAT_WIDTH) ** 2))
    dissipated_power = HEAT_GAIN * sliding_traction * sliding_speed
    heat_level_change = (
        HEAT_DIFFUSIVITY * discrete_laplacian(heat_level)
        + across_layout[:, None, None] * dissipated_power[None]
    )
    fluid_load_change = (
        FLUID_DIFFUSIVITY * discrete_laplacian(fluid_load) + FLUID_TOGGLE * heat_level_change
    )
    memory_change = healing_effect_b * (
        jnp.exp((REF_FRICTION - contact_memory) / healing_effect_b) - sliding_speed
    )
    extra_contribution = (
        friction * fluid_load_change[0] - effective * (sliding_speed / root_term) * memory_change
    )
    denominator_value = effective * instant_effect_a / root_term + DAMPING
    return (
        extra_contribution,
        denominator_value,
        sliding_traction,
        memory_change,
        heat_level_change,
        fluid_load_change,
    )


def kernel_table(rows_index, cols_index, depth_total, strike_total):
    depth_mode = jnp.minimum(rows_index, depth_total - rows_index).astype(jnp.float32)
    strike_mode = jnp.minimum(cols_index, strike_total - cols_index).astype(jnp.float32)
    depth_wave = 2.0 * math.pi / depth_total * depth_mode
    strike_wave = 2.0 * math.pi / strike_total * strike_mode
    wave_square = strike_wave * strike_wave + depth_wave * depth_wave
    return (
        -0.5
        * (strike_wave * strike_wave * ELASTIC + depth_wave * depth_wave)
        / jnp.sqrt(jnp.where(wave_square > 0, wave_square, 1.0))
    )


def trig_pair(left_index, right_index, modulus):
    phase_angle = 2.0 * math.pi / modulus * (left_index * right_index % modulus).astype(jnp.float32)
    return (jnp.cos(phase_angle), jnp.sin(phase_angle))


def depth_columns(fields):
    return lax.all_to_all(fields, "depth", split_axis=2, concat_axis=1, tiled=True)


def depth_rows(columns):
    return lax.all_to_all(columns, "depth", split_axis=1, concat_axis=2, tiled=True)


def depth_cas(columns, depth_total):
    depth_index = jnp.arange(depth_total, dtype=jnp.int32)
    cosine, sine_part = trig_pair(depth_index[:, None], depth_index[None, :], depth_total)
    return jnp.einsum("gz,fzw->fgw", cosine + sine_part, columns, precision=HIGHEST)


def six_step_filter(fields):
    strike_count = lax.axis_size("strike")
    strike_pos = lax.axis_index("strike")
    depth_count = lax.axis_size("depth")
    depth_pos = lax.axis_index("depth")
    field_count, rows_local, cells_local = fields.shape
    block_width = cells_local // strike_count
    strike_total = cells_local * strike_count
    depth_total = rows_local * depth_count
    sub_width = cells_local // depth_count
    received = lax.all_to_all(
        fields.reshape(field_count, rows_local, strike_count, block_width),
        "strike",
        split_axis=2,
        concat_axis=2,
        tiled=True,
    )
    strike_index = jnp.arange(strike_count, dtype=jnp.int32)
    cos_one, sin_one = trig_pair(strike_index[:, None], strike_index[None, :], strike_count)
    first_re = jnp.einsum("kn,fznl->fzkl", cos_one, received, precision=HIGHEST)
    first_im = -jnp.einsum("kn,fznl->fzkl", sin_one, received, precision=HIGHEST)
    gathered = lax.all_to_all(
        jnp.stack([first_re, first_im], 1), "strike", split_axis=3, concat_axis=3, tiled=True
    )
    cell_index = (
        strike_index[:, None] * block_width + jnp.arange(block_width, dtype=jnp.int32)[None, :]
    )
    wave_index = strike_pos + strike_count * jnp.arange(cells_local, dtype=jnp.int32)
    cos_two, sin_two = trig_pair(cell_index[:, :, None], wave_index[None, None, :], strike_total)
    spectrum = jnp.einsum(
        "fzgl,glj->fzj", gathered[:, 0], cos_two + sin_two, precision=HIGHEST
    ) + jnp.einsum("fzgl,glj->fzj", gathered[:, 1], sin_two - cos_two, precision=HIGHEST)
    columns = depth_columns(spectrum)
    depth_spec = depth_cas(columns, depth_total)
    local_wave = lax.dynamic_slice_in_dim(wave_index, depth_pos * sub_width, sub_width)
    depth_index = jnp.arange(depth_total, dtype=jnp.int32)
    kernel = kernel_table(depth_index[:, None], local_wave[None, :], depth_total, strike_total) / (
        depth_total * strike_total
    )
    restored = depth_cas(depth_spec * kernel[None], depth_total)
    filtered = depth_rows(restored)
    back_re = jnp.einsum("fzj,glj->fzgl", filtered, cos_two, precision=HIGHEST)
    back_im = -jnp.einsum("fzj,glj->fzgl", filtered, sin_two, precision=HIGHEST)
    regrouped = lax.all_to_all(
        jnp.stack([back_re, back_im], 1), "strike", split_axis=3, concat_axis=3, tiled=True
    )
    values = jnp.einsum(
        "fzsl,ns->fznl", regrouped[:, 0], cos_one + sin_one, precision=HIGHEST
    ) + jnp.einsum("fzsl,ns->fznl", regrouped[:, 1], sin_one - cos_one, precision=HIGHEST)
    arrived = lax.all_to_all(values, "strike", split_axis=2, concat_axis=2, tiled=True)
    return arrived.reshape(field_count, rows_local, cells_local)


def shards(
    sliding_speed,
    offset_displacement,
    contact_memory,
    clamping_traction,
    instant_effect_a,
    healing_effect_b,
    ambient_traction,
    heat_level,
    fluid_load,
):
    fields = jnp.stack([sliding_speed, offset_displacement])
    filtered = six_step_filter(fields)
    (
        extra_contribution,
        denominator_value,
        sliding_traction,
        memory_change,
        heat_level_change,
        fluid_load_change,
    ) = interface_tendencies(
        sliding_speed,
        contact_memory,
        clamping_traction,
        instant_effect_a,
        healing_effect_b,
        heat_level,
        fluid_load,
    )
    mismatch = ambient_traction + filtered[1] - DAMPING * sliding_speed - sliding_traction
    sliding_acceleration = (
        filtered[0] + extra_contribution + RELAXATION * mismatch
    ) / denominator_value
    return (sliding_acceleration, memory_change, heat_level_change, fluid_load_change)


def solution(mesh):
    in_specs = (
        P("depth", "strike"),
        P("depth", "strike"),
        P("depth", "strike"),
        P("depth", "strike"),
        P("depth", "strike"),
        P("depth", "strike"),
        P("depth", "strike"),
        P(None, "depth", "strike"),
        P(None, "depth", "strike"),
    )
    out_specs = (
        P("depth", "strike"),
        P("depth", "strike"),
        P(None, "depth", "strike"),
        P(None, "depth", "strike"),
    )
    return jax.shard_map(shards, mesh=mesh, in_specs=in_specs, out_specs=out_specs, check_vma=False)
```

profile of v0, /device:TPU:1, one launch (start us, length us, event | category | flops | bytes accessed | tf_op | source)
XLA Modules:
  0.0 171.3 jit_solution(5020923376332547622)
XLA Ops:
  2.7 22.8 %all_to_all.56 = f32[2,96,32,8]{1,3,0,2:T(8,128)S(1)} all-to-all(f32[2,96,32,8]{1,3,0,2:T(8,128)S(1)} %copy.106), channel_id=1, replica_groups=mesh['strike'=32,'depth'=8] {'strike'}, dimensions={2} | all-to-all | bytes 393216 | tf_op jit(solution)/shard_map/all_to_all | solution.py:111
  26.4 1.1 copy.109
  27.5 5.0 %all-to-all-start.1 = ((f32[2,2,96,32,8]{2,4,0,1,3:T(8,128)}), f32[2,2,96,32,8]{2,4,0,1,3:T(8,128)S(1)}, u32[]{:S(2)}, u32[]{:S(2)}) async-start(f32[2,2,96,32,8]{2,4,0,1,3:T(8,128)} %copy.109), calls=%async_computation.1 | async-start | bytes 1048576 | tf_op jit(solution)/shard_map/all_to_all | solution.py:122
  32.7 16.6 %all-to-all-done.1 = f32[2,2,96,32,8]{2,4,0,1,3:T(8,128)S(1)} async-done(((f32[2,2,96,32,8]{2,4,0,1,3:T(8,128)}), f32[2,2,96,32,8]{2,4,0,1,3:T(8,128)S(1)}, u32[]{:S(2)}, u32[]{:S(2)}) %all-to-all-start.1) | async-done | bytes 393248 | tf_op jit(solution)/shard_map/all_to_all | solution.py:122
  49.4 1.6 convolution_bitcast_fusion.2
  50.9 1.6 fusion.28
  53.4 6.4 %all-to-all-start.2 = ((f32[2,96,256]{1,0,2:T(2,128)}), f32[2,96,256]{1,0,2:T(2,128)S(1)}, u32[]{:S(2)}, u32[]{:S(2)}) async-start(f32[2,96,256]{1,0,2:T(2,128)} %copy.112), calls=%async_computation.2 | async-start | bytes 524288 | tf_op jit(solution)/shard_map/all_to_all | solution.py:88
  59.8 7.6 %all-to-all-done.2 = f32[2,96,256]{1,0,2:T(2,128)S(1)} async-done(((f32[2,96,256]{1,0,2:T(2,128)}), f32[2,96,256]{1,0,2:T(2,128)S(1)}, u32[]{:S(2)}, u32[]{:S(2)}) %all-to-all-start.2) | async-done | bytes 196640 | tf_op jit(solution)/shard_map/all_to_all | solution.py:88
  67.7 12.0 %fusion.29 = f32[2,768,32]{1,2,0:T(8,128)S(1)} fusion(f32[2,768,32]{1,2,0:T(8,128)S(1)} %all_to_all.43, f32[768,32]{0,1:T(8,128)S(1)} %fusion.54), kind=kOutput, calls=%fused_computation.37 | convolution fusion | flops 458932224 | bytes 491520 | tf_op jit(solution)/shard_map/gz,fzw->fgw/dot_general | solution.py:98
  79.8 12.0 %fusion.25 = f32[2,768,32]{1,2,0:T(8,128)S(1)} fusion(f32[2,768,32]{1,2,0:T(8,128)S(1)} %fusion.29), kind=kOutput, calls=%fused_computation.35 | convolution fusion | flops 458883072 | bytes 393216 | tf_op jit(solution)/shard_map/gz,fzw->fgw/dot_general | solution.py:98
  91.9 1.1 copy.115
  93.0 2.6 %reshape.153 = f32[8,1,6144]{2,1,0:T(1,128)} reshape(f32[768,2,32]{2,1,0:T(2,128)} %bitcast.129) | data formatting | bytes 393216
  95.6 3.6 %all-to-all-start.3 = ((f32[8,1,6144]{2,1,0:T(1,128)}), f32[8,1,6144]{2,1,0:T(1,128)S(1)}, u32[]{:S(2)}, u32[]{:S(2)}) async-start(f32[8,1,6144]{2,1,0:T(1,128)} %reshape.153), calls=%async_computation.3 | async-start | bytes 393216 | tf_op jit(solution)/shard_map/all_to_all | solution.py:92
  99.2 1.1 multiply_multiply_fusion
  100.3 5.9 %all-to-all-done.3 = f32[8,1,6144]{2,1,0:T(1,128)S(1)} async-done(((f32[8,1,6144]{2,1,0:T(1,128)}), f32[8,1,6144]{2,1,0:T(1,128)S(1)}, u32[]{:S(2)}, u32[]{:S(2)}) %all-to-all-start.3) | async-done | bytes 196640 | tf_op jit(solution)/shard_map/all_to_all | solution.py:92
  106.7 1.8 %reduce = f32[8,6144]{1,0:T(8,128)} reduce(f32[8,1,6144]{2,1,0:T(1,128)S(1)} %all-to-all-done.3, f32[]{:T(128)} %broadcast.205), dimensions={1}, to_apply=%all_to_all.44.reduce_sub_computation | reduce | bytes 393220 | tf_op jit(solution)/shard_map/all_to_all | solution.py:92
  108.5 2.5 %reshape.154 = f32[768,2,32]{2,1,0:T(2,128)} reshape(f32[8,6144]{1,0:T(8,128)} %reduce) | data formatting | bytes 393216
  111.0 2.0 %copy.116 = f32[2,8,96,32]{2,3,1,0:T(8,128)} copy(f32[2,8,96,32]{3,0,2,1:T(2,128)} %bitcast.130) | data formatting | bytes 393216 | tf_op jit(solution)/shard_map/all_to_all | solution.py:92
  113.0 2.4 %fusion.20 = f32[2,1,96,32,8]{2,3,4,0,1:T(8,128)S(1)} fusion(f32[2,96,256,1]{1,2,3,0:T(8,128)} %bitcast.134, s32[256]{0:T(256)S(1)} %multiply_add_fusion, s32[32,8]{0,1:T(8,128)S(1)} %iota_add_fusion), kind=kOutput, calls=%fused_computation.27 | convolution fusion | flops 151961600 | bytes 395264 | tf_op jit(solution)/shard_map/fzj,glj->fzgl/dot_general | solution.py:143
  115.3 2.3 %convolution_bitcast_fusion = f32[2,1,96,32,8]{2,3,4,0,1:T(8,128)S(1)} fusion(f32[2,96,256,1]{1,2,3,0:T(8,128)} %bitcast.135, s32[256]{0:T(256)S(1)} %multiply_add_fusion, s32[32,8]{0,1:T(8,128)S(1)} %iota_add_fusion), kind=kOutput, calls=%fused_computation.28 | convolution fusion | flops 151912448 | bytes 395264 | tf_op jit(solution)/shard_map/fzj,glj->fzgl/dot_general | solution.py:142
  117.7 1.1 copy.119
  118.8 8.7 %all-to-all-start.4 = ((f32[2,2,96,32,8]{2,4,0,1,3:T(8,128)}), f32[2,2,96,32,8]{2,4,0,1,3:T(8,128)}, u32[]{:S(2)}, u32[]{:S(2)}) async-start(f32[2,2,96,32,8]{2,4,0,1,3:T(8,128)} %copy.119), calls=%async_computation.4 | async-start | bytes 1048576 | tf_op jit(solution)/shard_map/all_to_all | solution.py:144
  127.6 7.8 %fusion.126 = (f32[31,96,256]{2,1,0:T(8,128)}, f32[31,96,256]{2,1,0:T(8,128)}, f32[31,96,256]{2,1,0:T(8,128)}, f32[31,96,256]{2,1,0:T(8,128)}) fusion(f32[32,96,256]{2,1,0:T(8,128)} %param.16, f32[32,96,256]{2,1,0:T(8,128)S(1)} %copy-done), kind=kLoop, calls=%fused_computation.148 | loop fusion | bytes 24379392 | tf_op jit(solution)/shard_map/slice | solution.py:21
  135.4 9.0 %all-to-all-done.4 = f32[2,2,96,32,8]{2,4,0,1,3:T(8,128)} async-done(((f32[2,2,96,32,8]{2,4,0,1,3:T(8,128)}), f32[2,2,96,32,8]{2,4,0,1,3:T(8,128)}, u32[]{:S(2)}, u32[]{:S(2)}) %all-to-all-start.4) | async-done | bytes 393248 | tf_op jit(solution)/shard_map/all_to_all | solution.py:144
  144.3 1.1 fusion.128
  147.2 6.2 %all-to-all-start.5 = ((f32[2,96,32,8]{1,3,0,2:T(8,128)}), f32[2,96,32,8]{1,3,0,2:T(8,128)}, u32[]{:S(2)}, u32[]{:S(2)}) async-start(f32[2,96,32,8]{1,3,0,2:T(8,128)} %copy.122), calls=%async_computation.5 | async-start | bytes 524288 | tf_op jit(solution)/shard_map/all_to_all | solution.py:150
  153.5 8.3 %fusion.1 = (f32[32,96,256]{2,1,0:T(8,128)}, f32[32,96,256]{2,1,0:T(8,128)}) fusion(f32[31,96,256]{2,1,0:T(8,128)} %get-tuple-element.28, f32[1,96,256]{2,1,0:T(8,128)S(1)} %slice-done, f32[32,96,256]{2,1,0:T(8,128)S(1)} %copy-done.1, f32[31,96,256]{2,1,0:T(8,128)} %get-tuple-element.29, f32[96,256]{1,0:T(8,128)S(1)} %multiply_multiply_fusion, ...), kind=kLoop, calls=%fused_computation.3 | loop fusion | flops 11010048 | bytes 25067648 | tf_op jit(solution)/shard_map/add | solution.py:50
  161.8 3.7 %all-to-all-done.5 = f32[2,96,32,8]{1,3,0,2:T(8,128)} async-done(((f32[2,96,32,8]{1,3,0,2:T(8,128)}), f32[2,96,32,8]{1,3,0,2:T(8,128)}, u32[]{:S(2)}, u32[]{:S(2)}) %all-to-all-start.5) | async-done | bytes 196640 | tf_op jit(solution)/shard_map/all_to_all | solution.py:150
  165.6 1.7 slice_bitcast_fusion
  167.3 1.0 copy.124
  168.3 1.0 copy.123
  169.3 2.0 %fusion.59 = (f32[96,256]{1,0:T(8,128)}, f32[96,256]{1,0:T(8,128)}) fusion(f32[96,256]{1,0:T(8,128)S(1)} %copy.123, f32[32,96,256]{2,1,0:T(8,128)} %get-tuple-element.14, f32[96,256]{1,0:T(8,128)} %param.13, f32[96,256]{1,0:T(8,128)} %param.15, f32[96,256]{1,0:T(8,128)S(1)} %copy.124, f32[96,256]{1,0:T(8,128)S(1)} %copy-done.2, f32[96,256]{1,0:T(8,128)} %param.11, ...), kind=kLoop, calls=%fused_computation.75 | loop fusion | flops 811008 | bytes 1179648 | tf_op jit(solution)/shard_map/div | solution.py:184
  (34 shorter events, 6.8 us)
Async XLA Ops:
  27.5 21.8 %all-to-all-start.1 = ((f32[2,2,96,32,8]{2,4,0,1,3:T(8,128)}), f32[2,2,96,32,8]{2,4,0,1,3:T(8,128)S(1)}, u32[]{:S(2)}, u32[]{:S(2)}) async-start(f32[2,2,96,32,8]{2,4,0,1,3:T(8,128)} %copy.109), calls=%async_computation.1 | async-start | bytes 1048576 | tf_op jit(solution)/shard_map/all_to_all | solution.py:122
  53.4 14.1 %all-to-all-start.2 = ((f32[2,96,256]{1,0,2:T(2,128)}), f32[2,96,256]{1,0,2:T(2,128)S(1)}, u32[]{:S(2)}, u32[]{:S(2)}) async-start(f32[2,96,256]{1,0,2:T(2,128)} %copy.112), calls=%async_computation.2 | async-start | bytes 524288 | tf_op jit(solution)/shard_map/all_to_all | solution.py:88
  79.8 19.4 %copy-start = (f32[32,96,256]{2,1,0:T(8,128)S(1)}, f32[32,96,256]{2,1,0:T(8,128)}, u32[]{:S(2)}) copy-start(f32[32,96,256]{2,1,0:T(8,128)} %param.17) | copy-start | bytes 9437188
  79.8 19.4 %copy-start.2 = (f32[96,256]{1,0:T(8,128)S(1)}, f32[96,256]{1,0:T(8,128)}, u32[]{:S(2)}) copy-start(f32[96,256]{1,0:T(8,128)} %param.9) | copy-start | bytes 294916
  95.6 10.6 %all-to-all-start.3 = ((f32[8,1,6144]{2,1,0:T(1,128)}), f32[8,1,6144]{2,1,0:T(1,128)S(1)}, u32[]{:S(2)}, u32[]{:S(2)}) async-start(f32[8,1,6144]{2,1,0:T(1,128)} %reshape.153), calls=%async_computation.3 | async-start | bytes 393216 | tf_op jit(solution)/shard_map/all_to_all | solution.py:92
  118.8 25.5 %all-to-all-start.4 = ((f32[2,2,96,32,8]{2,4,0,1,3:T(8,128)}), f32[2,2,96,32,8]{2,4,0,1,3:T(8,128)}, u32[]{:S(2)}, u32[]{:S(2)}) async-start(f32[2,2,96,32,8]{2,4,0,1,3:T(8,128)} %copy.119), calls=%async_computation.4 | async-start | bytes 1048576 | tf_op jit(solution)/shard_map/all_to_all | solution.py:144
  135.4 18.1 %copy-start.1 = (f32[32,96,256]{2,1,0:T(8,128)S(1)}, f32[32,96,256]{2,1,0:T(8,128)}, u32[]{:S(2)}) copy-start(f32[32,96,256]{2,1,0:T(8,128)} %param.17) | copy-start | bytes 9437188
  135.4 18.1 %slice-start = ((f32[32,96,256]{2,1,0:T(8,128)}), f32[1,96,256]{2,1,0:T(8,128)S(1)}, s32[]{:S(2)}) async-start(f32[32,96,256]{2,1,0:T(8,128)} %param.17), calls=%async_computation.6 | async-start | bytes 196608 | tf_op jit(solution)/shard_map/slice | solution.py:22
  135.4 18.2 %slice-start.1 = ((f32[32,96,256]{2,1,0:T(8,128)}), f32[1,96,256]{2,1,0:T(8,128)S(1)}, s32[]{:S(2)}) async-start(f32[32,96,256]{2,1,0:T(8,128)} %param.16), calls=%async_computation.7 | async-start | bytes 196608 | tf_op jit(solution)/shard_map/slice | solution.py:22
  147.2 18.3 %all-to-all-start.5 = ((f32[2,96,32,8]{1,3,0,2:T(8,128)}), f32[2,96,32,8]{1,3,0,2:T(8,128)}, u32[]{:S(2)}, u32[]{:S(2)}) async-start(f32[2,96,32,8]{1,3,0,2:T(8,128)} %copy.122), calls=%async_computation.5 | async-start | bytes 524288 | tf_op jit(solution)/shard_map/all_to_all | solution.py:150
where the time goes:
time: 172 us; the launch traced here: 171 us
  waiting for transfers between devices  42.8 us (25%)
  matrix products  33.8 us (20%)
  starting transfers between devices  30 us (17%)
  local copies, waits for them, and re-layouts  27.4 us (16%)
  blocking collectives  22.8 us (13%)
  other arithmetic  13.5 us (8%)
    dot_general x2, matrix products, depth_cas(): jnp.einsum('gz,fzw->fgw', cosine + sine_part, columns, precision=HIGHEST)  24.1 us
    all_to_all x1, blocking collectives, six_step_filter(): lax.all_to_all(fields.reshape(field_count, rows_local, strike_count, bloc...  22.8 us
    all_to_all x1, waiting for transfers between devices, six_step_filter(): lax.all_to_all(jnp.stack([first_re, first_im], 1), 'strike', split_axis=3...  16.6 us
    all_to_all x1, waiting for transfers between devices, six_step_filter(): lax.all_to_all(jnp.stack([back_re, back_im], 1), 'strike', split_axis=3,...  8.96 us
    all_to_all x1, starting transfers between devices, six_step_filter(): lax.all_to_all(jnp.stack([back_re, back_im], 1), 'strike', split_axis=3,...  8.72 us
    add x1, other arithmetic, interface_tendencies(): FLUID_DIFFUSIVITY * discrete_laplacian(fluid_load)  8.31 us
    slice x1, local copies, waits for them, and re-layouts, discrete_laplacian(): values_in[1:]  7.79 us
    all_to_all x1, waiting for transfers between devices, depth_columns(): lax.all_to_all(fields, 'depth', split_axis=2, concat_axis=1, tiled=True)  7.62 us
  transfers between devices with their start and end apart: 5, of which 5 were waited for; matrix products, arithmetic and copies ran while one was open for 10% of the time, Pallas kernels for 0%

commit v1 on v0

v1 whole, which is shorter than its diff:
```python
import math

import jax
import jax.numpy as jnp
import ml_dtypes
import numpy as np
from jax import lax
from jax.experimental import pallas as pl
from jax.experimental.pallas import tpu as pltpu
from jax.sharding import PartitionSpec as P

HEAT_GAIN = 0.05
HEAT_DIFFUSIVITY = 0.3
FLUID_DIFFUSIVITY = 0.45
FLUID_TOGGLE = 0.6
REF_FRICTION = 0.5
DAMPING = 0.5
RELAXATION = 0.2
ELASTIC = 4.0 / 3.0
HEAT_WIDTH = 4.0

DEPTH = 768
STRIKE = 8192
ROWS = 96
COLS = 256
POINTS = 32
DEPTH_PARTS = 8
STRIKE_PARTS = 32
LANES = 128
COARSE = STRIKE // LANES
CLASSES = COARSE // 2 + 1
MODES = 3
SLOTS = 4
SPEC_ROWS = 112

F32 = jnp.float32
BF16 = jnp.bfloat16


def halves(table):
    high = table.astype(ml_dtypes.bfloat16)
    low = (table - high.astype(np.float64)).astype(ml_dtypes.bfloat16)
    return high, low


def depth_table():
    index = np.arange(DEPTH)
    angle = 2.0 * np.pi / DEPTH * (index[:, None] * index[None, :] % DEPTH)
    return np.cos(angle) + np.sin(angle)


def coarse_tables():
    angle = 2.0 * np.pi / COARSE * (np.arange(CLASSES)[:, None] * np.arange(COARSE)[None, :] % COARSE)
    forward = np.zeros((2, SPEC_ROWS, COARSE, SLOTS))
    inverse = np.zeros((COARSE, SLOTS, 2, SPEC_ROWS))
    weight = np.where(np.arange(CLASSES) % (COARSE // 2) == 0, 1.0, 2.0)[:, None]
    for mode in range(MODES):
        at = np.arange(CLASSES) * MODES + mode
        forward[0, at, :, mode] = np.cos(angle)
        forward[1, at, :, mode] = -np.sin(angle)
        inverse[:, mode, 0, at] = (weight * np.cos(angle)).T
        inverse[:, mode, 1, at] = (-weight * np.sin(angle)).T
    return (
        forward.reshape(2 * SPEC_ROWS, COARSE * SLOTS),
        inverse.reshape(COARSE * SLOTS, 2 * SPEC_ROWS),
    )


def fine_tables():
    index = np.arange(LANES)
    angle = 2.0 * np.pi / LANES * (index[:, None] * index[None, :] % LANES)
    cosine, sine = np.cos(angle), np.sin(angle)
    forward = np.block([[cosine, -sine], [sine, cosine]])
    inverse = np.block([[cosine, sine], [-sine, cosine]])
    return forward, inverse


def class_tables():
    row = np.arange(SPEC_ROWS)
    k_one = np.minimum(row // MODES, CLASSES - 1)
    lane = np.arange(LANES)
    angle = 2.0 * np.pi / STRIKE * (k_one[:, None] * lane[None, :])
    wave = k_one[:, None] + COARSE * lane[None, :]
    strike_wave = 2.0 * np.pi / STRIKE * np.minimum(wave, STRIKE - wave)
    offset = np.broadcast_to((row % MODES * STRIKE_PARTS)[:, None], (SPEC_ROWS, LANES))
    return tuple(
        np.asarray(table, np.float32)
        for table in (np.cos(angle), np.sin(angle), strike_wave * strike_wave, offset)
    )


def split(values):
    high = values.astype(BF16)
    return high, (values - high.astype(F32)).astype(BF16)


def mm(left, right):
    return jnp.dot(left, right, preferred_element_type=F32)


def table_first(high, low, values):
    v_high, v_low = split(values)
    return mm(high, v_high) + (mm(high, v_low) + mm(low, v_high))


def table_last(values, high, low):
    v_high, v_low = split(values)
    return mm(v_high, high) + (mm(v_low, high) + mm(v_high, low))


def depth_kernel(fields_ref, high_ref, low_ref, out_ref):
    modes = table_first(high_ref[...], low_ref[...], fields_ref[...])
    blank = jnp.zeros((STRIKE_PARTS, LANES), F32)
    for half in range(2):
        for slot in range(SLOTS):
            piece = blank
            if slot < MODES:
                piece = modes[
                    slot * STRIKE_PARTS : (slot + 1) * STRIKE_PARTS,
                    half * LANES : (half + 1) * LANES,
                ]
            out_ref[pl.ds(half * SLOTS + slot, STRIKE_PARTS, stride=2 * SLOTS), :] = piece


def strike_kernel(
    base_ref,
    modes_ref,
    coarse_high,
    coarse_low,
    fine_high,
    fine_low,
    back_high,
    back_low,
    out_high,
    out_low,
    cos_ref,
    sin_ref,
    strike_square_ref,
    offset_ref,
    out_ref,
):
    cosine, sine = cos_ref[...], sin_ref[...]
    depth_index = offset_ref[...] + base_ref[0].astype(F32)
    depth_wave = 2.0 * math.pi / DEPTH * jnp.minimum(depth_index, DEPTH - depth_index)
    depth_square = depth_wave * depth_wave
    strike_square = strike_square_ref[...]
    wave_square = strike_square + depth_square
    kernel = (
        (-0.5 / (DEPTH * STRIKE))
        * (strike_square * ELASTIC + depth_square)
        / jnp.sqrt(jnp.where(wave_square > 0, wave_square, 1.0))
    )
    coarse = table_first(coarse_high[...], coarse_low[...], modes_ref[...])
    real, imag = coarse[:SPEC_ROWS], coarse[SPEC_ROWS:]
    turned = jnp.concatenate([real * cosine + imag * sine, imag * cosine - real * sine], 1)
    spectrum = table_last(turned, fine_high[...], fine_low[...])
    spectrum = spectrum * jnp.concatenate([kernel, kernel], 1)
    back = table_last(spectrum, back_high[...], back_low[...])
    real, imag = back[:, :LANES], back[:, LANES:]
    turned = jnp.concatenate([real * cosine - imag * sine, imag * cosine + real * sine], 0)
    out_ref[...] = table_first(out_high[...], out_low[...], turned)


def spread_kernel(modes_ref, out_ref):
    for half in range(2):
        for slot in range(MODES):
            piece = modes_ref[pl.ds(half * SLOTS + slot, STRIKE_PARTS, stride=2 * SLOTS), :]
            for part in range(DEPTH_PARTS):
                out_ref[
                    part,
                    slot * STRIKE_PARTS : (slot + 1) * STRIKE_PARTS,
                    half * LANES : (half + 1) * LANES,
                ] = piece


def final_kernel(modes_ref, high_ref, low_ref, numerator_ref, denominator_ref, out_ref):
    filtered = table_first(high_ref[...], low_ref[...], modes_ref[...])
    out_ref[...] = (filtered + numerator_ref[...]) / denominator_ref[...]


def heat_kernel(
    speed_ref,
    memory_ref,
    clamping_ref,
    effect_a_ref,
    effect_b_ref,
    ambient_ref,
    heat_ref,
    fluid_ref,
    heat_out,
    memory_out,
    numerator_out,
    denominator_out,
):
    speed, memory = speed_ref[...], memory_ref[...]
    effect_a, effect_b = effect_a_ref[...], effect_b_ref[...]
    ratio = memory / effect_a
    argument = 0.5 * speed * jnp.exp(ratio)
    friction = effect_a * jnp.log(argument + jnp.sqrt(argument * argument + 1.0))
    root_term = jnp.sqrt(4.0 * jnp.exp(-2.0 * ratio) + speed * speed)
    effective = clamping_ref[...] - fluid_ref[0]
    traction = effective * friction
    power = HEAT_GAIN * traction * speed
    memory_change = effect_b * (jnp.exp((REF_FRICTION - memory) / effect_b) - speed)
    memory_out[...] = memory_change
    for point in range(POINTS):
        here = heat_ref[point]
        above = heat_ref[point + 1] if point + 1 < POINTS else None
        below = heat_ref[point - 1] if point > 0 else heat_ref[1]
        bent = below - 2.0 * here
        if above is not None:
            bent = bent + above
        change = HEAT_DIFFUSIVITY * bent + math.exp(-((point / HEAT_WIDTH) ** 2)) * power
        heat_out[point] = change
        if point == 0:
            fluid_change = (
                FLUID_DIFFUSIVITY * (2.0 * fluid_ref[1] - 2.0 * fluid_ref[0])
                + FLUID_TOGGLE * change
            )
    extra = friction * fluid_change - effective * (speed / root_term) * memory_change
    numerator_out[...] = extra + RELAXATION * (ambient_ref[...] - DAMPING * speed - traction)
    denominator_out[...] = effective * effect_a / root_term + DAMPING


def fluid_kernel(fluid_ref, heat_change_ref, out_ref):
    for point in range(POINTS):
        here = fluid_ref[point]
        below = fluid_ref[point - 1] if point > 0 else fluid_ref[1]
        bent = below - 2.0 * here
        if point + 1 < POINTS:
            bent = bent + fluid_ref[point + 1]
        out_ref[point] = FLUID_DIFFUSIVITY * bent + FLUID_TOGGLE * heat_change_ref[point]


def whole(count):
    return [pl.BlockSpec(memory_space=pltpu.VMEM)] * count


def cost(flops, moved):
    return pl.CostEstimate(flops=flops, bytes_accessed=moved, transcendentals=0)


def shape(*dims):
    return jax.ShapeDtypeStruct(dims, F32)


BLOCK = 16


def rows_spec():
    return pl.BlockSpec((BLOCK, COLS), lambda i: (i, 0))


def points_spec(points=POINTS):
    return pl.BlockSpec((points, BLOCK, COLS), lambda i: (0, i, 0))


def shards(
    sliding_speed,
    offset_displacement,
    contact_memory,
    clamping_traction,
    instant_effect_a,
    healing_effect_b,
    ambient_traction,
    heat_level,
    fluid_load,
):
    depth_pos = lax.axis_index("depth")
    strike_pos = lax.axis_index("strike")
    depth_high, depth_low = (
        lax.dynamic_slice_in_dim(jnp.asarray(table), depth_pos * ROWS, ROWS, 0)
        for table in halves(depth_table())
    )
    coarse_forward, coarse_inverse = coarse_tables()
    fine_forward, fine_inverse = fine_tables()
    base = (depth_pos * ROWS + strike_pos).astype(jnp.int32).reshape(1)
    small = ROWS * COLS * 4

    field = sliding_speed + RELAXATION * offset_displacement
    sent = jnp.broadcast_to(field[None], (DEPTH_PARTS, ROWS, COLS))
    columns = lax.all_to_all(sent, "depth", split_axis=0, concat_axis=0)

    modes = pl.pallas_call(
        depth_kernel,
        out_shape=shape(STRIKE_PARTS * 2 * SLOTS, LANES),
        in_specs=whole(3),
        out_specs=pl.BlockSpec(memory_space=pltpu.VMEM),
        cost_estimate=cost(6 * ROWS * DEPTH * COLS, 12 * small),
    )(columns.reshape(DEPTH, COLS), depth_high, depth_low)

    modes = lax.all_to_all(
        modes.reshape(STRIKE_PARTS, 2 * SLOTS, LANES), "strike", split_axis=0, concat_axis=0
    )

    filtered = pl.pallas_call(
        strike_kernel,
        out_shape=shape(STRIKE_PARTS * 2 * SLOTS, LANES),
        in_specs=[pl.BlockSpec(memory_space=pltpu.SMEM)] + whole(13),
        out_specs=pl.BlockSpec(memory_space=pltpu.VMEM),
        cost_estimate=cost(6 * 4 * 256 * 256 * LANES, 15 * small),
    )(
        base,
        modes.reshape(STRIKE_PARTS * 2 * SLOTS, LANES),
        *halves(coarse_forward),
        *halves(fine_forward),
        *halves(fine_inverse),
        *halves(coarse_inverse),
        *class_tables(),
    )

    filtered = lax.all_to_all(
        filtered.reshape(STRIKE_PARTS, 2 * SLOTS, LANES), "strike", split_axis=0, concat_axis=0
    )

    sent = pl.pallas_call(
        spread_kernel,
        out_shape=shape(DEPTH_PARTS, ROWS, COLS),
        in_specs=whole(1),
        out_specs=pl.BlockSpec(memory_space=pltpu.VMEM),
        cost_estimate=cost(0, 9 * small),
    )(filtered.reshape(STRIKE_PARTS * 2 * SLOTS, LANES))
    columns = lax.all_to_all(sent, "depth", split_axis=0, concat_axis=0)

    heat_level_change, memory_change, numerator, denominator = pl.pallas_call(
        heat_kernel,
        grid=(ROWS // BLOCK,),
        out_shape=(
            shape(POINTS, ROWS, COLS),
            shape(ROWS, COLS),
            shape(ROWS, COLS),
            shape(ROWS, COLS),
        ),
        in_specs=[rows_spec()] * 6 + [points_spec(), points_spec(2)],
        out_specs=(points_spec(), rows_spec(), rows_spec(), rows_spec()),
        cost_estimate=cost(8 * POINTS * ROWS * COLS, 75 * small),
    )(
        sliding_speed,
        contact_memory,
        clamping_traction,
        instant_effect_a,
        healing_effect_b,
        ambient_traction,
        heat_level,
        fluid_load,
    )
    fluid_load_change = pl.pallas_call(
        fluid_kernel,
        grid=(ROWS // BLOCK,),
        out_shape=shape(POINTS, ROWS, COLS),
        in_specs=[points_spec()] * 2,
        out_specs=points_spec(),
        cost_estimate=cost(8 * POINTS * ROWS * COLS, 96 * small),
    )(fluid_load, heat_level_change)

    sliding_acceleration = pl.pallas_call(
        final_kernel,
        out_shape=shape(ROWS, COLS),
        in_specs=whole(5),
        out_specs=pl.BlockSpec(memory_space=pltpu.VMEM),
        cost_estimate=cost(6 * ROWS * DEPTH * COLS, 14 * small),
    )(columns.reshape(DEPTH, COLS), depth_high, depth_low, numerator, denominator)
    return (sliding_acceleration, memory_change, heat_level_change, fluid_load_change)


def solution(mesh):
    plane = P("depth", "strike")
    block = P(None, "depth", "strike")
    return jax.shard_map(
        shards,
        mesh=mesh,
        in_specs=(plane,) * 7 + (block,) * 2,
        out_specs=(plane, plane, block, block),
        check_vma=False,
    )
```

time: 172 us -> 86.5 us (0.50)
  matrix products: 33.8 us -> 0 us
  waiting for transfers between devices: 42.8 us -> 18.7 us
  local copies, waits for them, and re-layouts: 27.4 us -> 5.08 us
  Pallas kernels: 0 us -> 21.3 us
  other arithmetic: 13.5 us -> 0.96 us
  blocking collectives: 22.8 us -> 15 us
  starting transfers between devices: 30 us -> 23.2 us
    dot_general x10 -> x0, matrix products: 33.8 us -> none  [the longest x2 24.1 us: depth_cas(): jnp.einsum('gz,fzw->fgw', cosine + sine_part, columns, precision=HIGHEST)]
    all_to_all x5 -> x3, waiting for transfers between devices: 42.8 us -> 18.7 us  [the longest x2 9.66 us: shards(): columns = lax.all_to_all(sent, 'depth', split_axis=0, concat_axis=0)]
    pallas_call x0 -> x6, Pallas kernels: none -> 21.3 us  [the longest x1 6.05 us: shards(): pl.pallas_call(fluid_kernel, grid=(ROWS // BLOCK,), out_shape=shape(POINT...]
    slice x7 -> x0, local copies, waits for them, and re-layouts: 8.91 us -> none  [the longest x1 7.79 us: discrete_laplacian(): values_in[1:]]
    all_to_all x1, blocking collectives: 22.8 us -> 15 us  [shards(): lax.all_to_all(filtered.reshape(STRIKE_PARTS, 2 * SLOTS, LANES), 'strike'...]
    add x3 -> x1, other arithmetic: 8.32 us -> 0.96 us  [shards(): field = sliding_speed + RELAXATION * offset_displacement]
    all_to_all x5 -> x3, starting transfers between devices: 30 us -> 23.2 us  [the longest x1 11.6 us: shards(): lax.all_to_all(modes.reshape(STRIKE_PARTS, 2 * SLOTS, LANES), 'strike', s...]
    unnamed x10 -> x6, local copies, waits for them, and re-layouts: 7.06 us -> 2.41 us
  transfers between devices with their start and end apart: 5 -> 3, of which waited for: 5 -> 2; matrix products, arithmetic and copies ran while one was open for 10% -> 2% of each run, Pallas kernels for 0% -> 14%
where the time goes in v1:
time: 86.5 us; the launch traced here: 84.9 us
  starting transfers between devices  23.2 us (27%)
  Pallas kernels  21.3 us (25%)
  waiting for transfers between devices  18.7 us (22%)
  blocking collectives  15 us (17%)
  local copies, waits for them, and re-layouts  5.08 us (6%)
  other arithmetic  0.96 us (1%)
    all_to_all x1, blocking collectives, shards(): lax.all_to_all(filtered.reshape(STRIKE_PARTS, 2 * SLOTS, LANES), 'strike'...  15 us
    all_to_all x1, starting transfers between devices, shards(): lax.all_to_all(modes.reshape(STRIKE_PARTS, 2 * SLOTS, LANES), 'strike', s...  11.6 us
    all_to_all x2, starting transfers between devices, shards(): columns = lax.all_to_all(sent, 'depth', split_axis=0, concat_axis=0)  11.5 us
    all_to_all x2, waiting for transfers between devices, shards(): columns = lax.all_to_all(sent, 'depth', split_axis=0, concat_axis=0)  9.66 us
    all_to_all x1, waiting for transfers between devices, shards(): lax.all_to_all(modes.reshape(STRIKE_PARTS, 2 * SLOTS, LANES), 'strike', s...  9.06 us
    pallas_call x1, Pallas kernels, shards(): pl.pallas_call(fluid_kernel, grid=(ROWS // BLOCK,), out_shape=shape(POINT...  6.05 us
    pallas_call x1, Pallas kernels, shards(): pl.pallas_call(heat_kernel, grid=(ROWS // BLOCK,), out_shape=(shape(POINT...  5.97 us
    pallas_call x1, Pallas kernels, shards(): pl.pallas_call(strike_kernel, out_shape=shape(STRIKE_PARTS * 2 * SLOTS, L...  2.94 us
  transfers between devices with their start and end apart: 3, of which 2 were waited for; matrix products, arithmetic and copies ran while one was open for 2% of the time, Pallas kernels for 14%

profile of v1, /device:TPU:1, one launch (start us, length us, event | category | flops | bytes accessed | tf_op | source)
XLA Modules:
  0.0 84.9 jit_solution(2704006048372471506)
XLA Ops:
  0.6 1.0 %multiply_add_fusion = f32[96,256]{1,0:T(8,128)S(1)} fusion(f32[96,256]{1,0:T(8,128)} %speed_ref.1, f32[96,256]{1,0:T(8,128)} %param.24), kind=kLoop, calls=%fused_computation | loop fusion | flops 49152 | bytes 294912 | tf_op jit(solution)/shard_map/add | solution.py:280
  1.6 0.9 %broadcast_in_dim.2 = f32[8,96,256]{2,1,0:T(8,128)} broadcast(f32[96,256]{1,0:T(8,128)S(1)} %multiply_add_fusion), dimensions={1,2} | broadcast | bytes 884736 | tf_op jit(solution)/shard_map/broadcast_in_dim | solution.py:281
  2.5 7.5 %all-to-all-start = ((f32[8,96,256]{2,1,0:T(8,128)}), f32[8,96,256]{2,1,0:T(8,128)S(1)}, u32[]{:S(2)}, u32[]{:S(2)}) async-start(f32[8,96,256]{2,1,0:T(8,128)} %broadcast_in_dim.2), calls=%async_computation | async-start | bytes 1572864 | tf_op jit(solution)/shard_map/all_to_all | solution.py:282
  10.0 1.7 %constant_dynamic-slice_fusion = (bf16[96,768]{1,0:T(8,128)(2,1)}, bf16[96,768]{1,0:T(8,128)(2,1)}) fusion(bf16[768,768]{1,0:T(8,128)(2,1)} %constant.46.clone, s32[]{:T(128)S(6)} %select_n.4, bf16[768,768]{1,0:T(8,128)(2,1)} %constant.45.clone), kind=kLoop, calls=%fused_computation.1 | loop fusion | bytes 589828 | tf_op jit(solution)/shard_map/dynamic_slice | solution.py:272
  11.7 9.7 %all-to-all-done = f32[8,96,256]{2,1,0:T(8,128)S(1)} async-done(((f32[8,96,256]{2,1,0:T(8,128)}), f32[8,96,256]{2,1,0:T(8,128)S(1)}, u32[]{:S(2)}, u32[]{:S(2)}) %all-to-all-start) | async-done | bytes 786464 | tf_op jit(solution)/shard_map/all_to_all | solution.py:282
  21.4 0.0 copy-start
  21.4 0.9 %copy-done = f32[8,96,256]{2,1,0:T(8,128)} copy-done((f32[8,96,256]{2,1,0:T(8,128)}, f32[8,96,256]{2,1,0:T(8,128)S(1)}, u32[]{:S(2)}) %copy-start) | copy-done | bytes 786456
  22.3 2.2 %shard_map.246 = f32[256,128]{1,0:T(8,128)} custom-call(f32[768,256]{1,0:T(8,128)} %bitcast.7, bf16[96,768]{1,0:T(8,128)(2,1)} %get-tuple-element.13.high_ref, bf16[96,768]{1,0:T(8,128)(2,1)} %get-tuple-element.12.low_ref), custom_call_target="tpu_custom_call" | custom-call | flops 113246208 | bytes 1179648 | tf_op jit(solution)/shard_map/pallas_call | solution.py:284
  24.5 11.6 %all-to-all-start.1 = ((f32[32,8,128]{2,1,0:T(8,128)}), f32[32,8,128]{2,1,0:T(8,128)S(1)}, u32[]{:S(2)}, u32[]{:S(2)}) async-start(f32[32,8,128]{2,1,0:T(8,128)} %bitcast.9), calls=%async_computation.1 | async-start | bytes 262144 | tf_op jit(solution)/shard_map/all_to_all | solution.py:292
  36.1 9.1 %all-to-all-done.1 = f32[32,8,128]{2,1,0:T(8,128)S(1)} async-done(((f32[32,8,128]{2,1,0:T(8,128)}), f32[32,8,128]{2,1,0:T(8,128)S(1)}, u32[]{:S(2)}, u32[]{:S(2)}) %all-to-all-start.1) | async-done | bytes 131104 | tf_op jit(solution)/shard_map/all_to_all | solution.py:292
  45.2 0.0 copy-start.2
  45.2 0.7 copy-done.2
  45.8 2.9 %shard_map.247 = f32[256,128]{1,0:T(8,128)} custom-call(s32[1]{0:T(128)} %bitcast.base_ref, f32[256,128]{1,0:T(8,128)} %bitcast.11, bf16[224,256]{1,0:T(8,128)(2,1)} %constant.47.clone.coarse_high, bf16[224,256]{1,0:T(8,128)(2,1)} %constant.48.clone.coarse_low, bf16[256,256]{1,0:T(8,128)(2,1)} %constant.49.clone.fine_high, ...), custom_call_target="tpu_custom_call" | custom-call | flops 201326592 | bytes 1474560 | tf_op jit(solution)/shard_map/pallas_call | solution.py:296
  48.8 15.0 %all_to_all.20 = f32[32,8,128]{2,1,0:T(8,128)} all-to-all(f32[32,8,128]{2,1,0:T(8,128)} %bitcast.12), channel_id=1, replica_groups=mesh['strike'=32,'depth'=8] {'strike'}, dimensions={0} | all-to-all | bytes 262144 | tf_op jit(solution)/shard_map/all_to_all | solution.py:312
  63.7 1.9 %shard_map.248 = f32[8,96,256]{2,1,0:T(8,128)} custom-call(f32[256,128]{1,0:T(8,128)} %bitcast.10), custom_call_target="tpu_custom_call" | custom-call | bytes 884736 | tf_op jit(solution)/shard_map/pallas_call | solution.py:316
  65.6 4.1 %all-to-all-start.3 = ((f32[8,96,256]{2,1,0:T(8,128)}), f32[8,96,256]{2,1,0:T(8,128)S(1)}, u32[]{:S(2)}, u32[]{:S(2)}) async-start(f32[8,96,256]{2,1,0:T(8,128)} %shard_map.248), calls=%async_computation.3 | async-start | bytes 1572864 | tf_op jit(solution)/shard_map/all_to_all | solution.py:323
  69.7 6.0 %shard_map.249 = (f32[32,96,256]{2,1,0:T(8,128)}, f32[96,256]{1,0:T(8,128)}, f32[96,256]{1,0:T(8,128)}, f32[96,256]{1,0:T(8,128)}) custom-call(f32[96,256]{1,0:T(8,128)} %speed_ref.1, f32[96,256]{1,0:T(8,128)} %memory_ref.1, f32[96,256]{1,0:T(8,128)} %clamping_ref.1, f32[96,256]{1,0:T(8,128)} %effect_a_ref.1, f32[96,256]{1,0:T(8,128)} %effect_b_ref.1, ...), custom_call_target="tpu_custom_call" | custom-call | flops 6291456 | bytes 7372800 | tf_op jit(solution)/shard_map/pallas_call | solution.py:325
  75.6 6.1 %shard_map.251 = f32[32,96,256]{2,1,0:T(8,128)} custom-call(f32[32,96,256]{2,1,0:T(8,128)} %fluid_ref.3, f32[32,96,256]{2,1,0:T(8,128)} %get-tuple-element.6.heat_change_ref), custom_call_target="tpu_custom_call" | custom-call | flops 6291456 | bytes 9437184 | tf_op jit(solution)/shard_map/pallas_call | solution.py:347
  81.7 0.0 all-to-all-done.3
  81.7 0.0 copy-start.1
  81.7 0.9 %copy-done.1 = f32[8,96,256]{2,1,0:T(8,128)} copy-done((f32[8,96,256]{2,1,0:T(8,128)}, f32[8,96,256]{2,1,0:T(8,128)S(1)}, u32[]{:S(2)}) %copy-start.1) | copy-done | bytes 786456
  82.6 2.3 %shard_map.250 = f32[96,256]{1,0:T(8,128)} custom-call(f32[768,256]{1,0:T(8,128)} %bitcast.8, bf16[96,768]{1,0:T(8,128)(2,1)} %get-tuple-element.13.high_ref, bf16[96,768]{1,0:T(8,128)(2,1)} %get-tuple-element.12.low_ref, f32[96,256]{1,0:T(8,128)} %get-tuple-element.8.numerator_ref, f32[96,256]{1,0:T(8,128)} %get-tuple-element.9.denominator_ref), custom_call_target="tpu_custom_call" | custom-call | flops 113246208 | bytes 1376256 | tf_op jit(solution)/shard_map/pallas_call | solution.py:356
Async XLA Ops:
  2.5 18.9 %all-to-all-start = ((f32[8,96,256]{2,1,0:T(8,128)}), f32[8,96,256]{2,1,0:T(8,128)S(1)}, u32[]{:S(2)}, u32[]{:S(2)}) async-start(f32[8,96,256]{2,1,0:T(8,128)} %broadcast_in_dim.2), calls=%async_computation | async-start | bytes 1572864 | tf_op jit(solution)/shard_map/all_to_all | solution.py:282
  21.4 0.9 %copy-start = (f32[8,96,256]{2,1,0:T(8,128)}, f32[8,96,256]{2,1,0:T(8,128)S(1)}, u32[]{:S(2)}) copy-start(f32[8,96,256]{2,1,0:T(8,128)S(1)} %all-to-all-done) | copy-start | bytes 2359300
  24.5 20.7 %all-to-all-start.1 = ((f32[32,8,128]{2,1,0:T(8,128)}), f32[32,8,128]{2,1,0:T(8,128)S(1)}, u32[]{:S(2)}, u32[]{:S(2)}) async-start(f32[32,8,128]{2,1,0:T(8,128)} %bitcast.9), calls=%async_computation.1 | async-start | bytes 262144 | tf_op jit(solution)/shard_map/all_to_all | solution.py:292
  45.2 0.7 copy-start.2
  65.6 16.1 %all-to-all-start.3 = ((f32[8,96,256]{2,1,0:T(8,128)}), f32[8,96,256]{2,1,0:T(8,128)S(1)}, u32[]{:S(2)}, u32[]{:S(2)}) async-start(f32[8,96,256]{2,1,0:T(8,128)} %shard_map.248), calls=%async_computation.3 | async-start | bytes 1572864 | tf_op jit(solution)/shard_map/all_to_all | solution.py:323
  81.7 0.9 %copy-start.1 = (f32[8,96,256]{2,1,0:T(8,128)}, f32[8,96,256]{2,1,0:T(8,128)S(1)}, u32[]{:S(2)}) copy-start(f32[8,96,256]{2,1,0:T(8,128)S(1)} %all-to-all-done.3) | copy-start | bytes 2359300

commit v2 on v1

v2 whole, which is shorter than its diff:
```python
import math

import jax
import jax.numpy as jnp
import ml_dtypes
import numpy as np
from jax import lax
from jax.experimental import pallas as pl
from jax.experimental.pallas import tpu as pltpu
from jax.sharding import PartitionSpec as P

HEAT_GAIN = 0.05
HEAT_DIFFUSIVITY = 0.3
FLUID_DIFFUSIVITY = 0.45
FLUID_TOGGLE = 0.6
REF_FRICTION = 0.5
DAMPING = 0.5
RELAXATION = 0.2
ELASTIC = 4.0 / 3.0
HEAT_WIDTH = 4.0

DEPTH = 768
STRIKE = 8192
ROWS = 96
COLS = 256
POINTS = 32
DEPTH_PARTS = 8
STRIKE_PARTS = 32
LANES = 128
COARSE = STRIKE // LANES
CLASSES = COARSE // 2 + 1
PAIRS = 4
PAIR_MODES = DEPTH // PAIRS
PAIR_SIZE = 2 * STRIKE_PARTS
MODES = 3
SLOTS = 4
SPEC_ROWS = 112

F32 = jnp.float32
BF16 = jnp.bfloat16


def halves(table):
    high = table.astype(ml_dtypes.bfloat16)
    low = (table - high.astype(np.float64)).astype(ml_dtypes.bfloat16)
    return high, low


def depth_table():
    index = np.arange(DEPTH)
    angle = 2.0 * np.pi / DEPTH * (index[:, None] * index[None, :] % DEPTH)
    return np.cos(angle) + np.sin(angle)


def depth_tables():
    table = depth_table()
    forward = table.reshape(PAIRS, PAIR_MODES, DEPTH)
    inverse = table.reshape(DEPTH, PAIRS, PAIR_MODES).transpose(1, 0, 2)
    return forward, inverse


def coarse_tables():
    angle = 2.0 * np.pi / COARSE * (np.arange(CLASSES)[:, None] * np.arange(COARSE)[None, :] % COARSE)
    forward = np.zeros((2, SPEC_ROWS, COARSE, SLOTS))
    inverse = np.zeros((COARSE, SLOTS, 2, SPEC_ROWS))
    weight = np.where(np.arange(CLASSES) % (COARSE // 2) == 0, 1.0, 2.0)[:, None]
    for mode in range(MODES):
        at = np.arange(CLASSES) * MODES + mode
        forward[0, at, :, mode] = np.cos(angle)
        forward[1, at, :, mode] = -np.sin(angle)
        inverse[:, mode, 0, at] = (weight * np.cos(angle)).T
        inverse[:, mode, 1, at] = (-weight * np.sin(angle)).T
    return (
        forward.reshape(2 * SPEC_ROWS, COARSE * SLOTS),
        inverse.reshape(COARSE * SLOTS, 2 * SPEC_ROWS),
    )


def fine_tables():
    index = np.arange(LANES)
    angle = 2.0 * np.pi / LANES * (index[:, None] * index[None, :] % LANES)
    cosine, sine = np.cos(angle), np.sin(angle)
    forward = np.block([[cosine, -sine], [sine, cosine]])
    inverse = np.block([[cosine, sine], [-sine, cosine]])
    return forward, inverse


def class_tables():
    row = np.arange(SPEC_ROWS)
    k_one = np.minimum(row // MODES, CLASSES - 1)
    lane = np.arange(LANES)
    angle = 2.0 * np.pi / STRIKE * (k_one[:, None] * lane[None, :])
    wave = k_one[:, None] + COARSE * lane[None, :]
    strike_wave = 2.0 * np.pi / STRIKE * np.minimum(wave, STRIKE - wave)
    offset = np.broadcast_to((row % MODES * PAIR_SIZE)[:, None], (SPEC_ROWS, LANES))
    return tuple(
        np.asarray(table, np.float32)
        for table in (np.cos(angle), np.sin(angle), strike_wave * strike_wave, offset)
    )


def split(values):
    high = values.astype(BF16)
    return high, (values - high.astype(F32)).astype(BF16)


def mm(left, right):
    return jnp.dot(left, right, preferred_element_type=F32)


def table_first(high, low, values):
    v_high, v_low = split(values)
    return mm(high, v_high) + (mm(high, v_low) + mm(low, v_high))


def table_last(values, high, low):
    v_high, v_low = split(values)
    return mm(v_high, high) + (mm(v_low, high) + mm(v_high, low))


def field_kernel(
    speed_hbm,
    slip_hbm,
    table_high,
    table_low,
    out_ref,
    high_out,
    low_out,
    speed_ref,
    slip_ref,
    sems,
):
    pair = lax.axis_index("depth") // 2
    loads = [
        pltpu.make_async_copy(source, target, sems.at[at])
        for at, (source, target) in enumerate(
            (
                (speed_hbm, speed_ref),
                (slip_hbm, slip_ref),
                (table_high.at[pair], high_out),
                (table_low.at[pair], low_out),
            )
        )
    ]
    for load in loads:
        load.start()
    loads[0].wait()
    loads[1].wait()
    field = speed_ref[...] + RELAXATION * slip_ref[...]
    for part in range(DEPTH_PARTS):
        half = part % 2
        out_ref[part] = field[:, half * LANES : (half + 1) * LANES]
    loads[2].wait()
    loads[3].wait()


def depth_kernel(fields_ref, high_ref, low_ref, out_ref):
    modes = table_first(high_ref[...], low_ref[...], fields_ref[...])
    for slot in range(SLOTS):
        piece = jnp.zeros((PAIR_SIZE, LANES), F32)
        if slot < MODES:
            piece = modes[slot * PAIR_SIZE : (slot + 1) * PAIR_SIZE]
        out_ref[pl.ds(slot, PAIR_SIZE, stride=SLOTS), :] = piece


def strike_kernel(
    modes_ref,
    coarse_high,
    coarse_low,
    fine_high,
    fine_low,
    back_high,
    back_low,
    out_high,
    out_low,
    cos_ref,
    sin_ref,
    strike_square_ref,
    offset_ref,
    out_ref,
):
    cosine, sine = cos_ref[...], sin_ref[...]
    depth_pos = lax.axis_index("depth")
    base = depth_pos // 2 * PAIR_MODES + 2 * lax.axis_index("strike") + depth_pos % 2
    depth_index = offset_ref[...] + base.astype(F32)
    depth_wave = 2.0 * math.pi / DEPTH * jnp.minimum(depth_index, DEPTH - depth_index)
    depth_square = depth_wave * depth_wave
    strike_square = strike_square_ref[...]
    wave_square = strike_square + depth_square
    kernel = (
        (-0.5 / (DEPTH * STRIKE))
        * (strike_square * ELASTIC + depth_square)
        / jnp.sqrt(jnp.where(wave_square > 0, wave_square, 1.0))
    )
    coarse = table_first(coarse_high[...], coarse_low[...], modes_ref[...])
    real, imag = coarse[:SPEC_ROWS], coarse[SPEC_ROWS:]
    turned = jnp.concatenate([real * cosine + imag * sine, imag * cosine - real * sine], 1)
    spectrum = table_last(turned, fine_high[...], fine_low[...])
    spectrum = spectrum * jnp.concatenate([kernel, kernel], 1)
    back = table_last(spectrum, back_high[...], back_low[...])
    real, imag = back[:, :LANES], back[:, LANES:]
    turned = jnp.concatenate([real * cosine - imag * sine, imag * cosine + real * sine], 0)
    out_ref[...] = table_first(out_high[...], out_low[...], turned)


def depth_back_kernel(modes_ref, high_ref, low_ref, out_ref):
    pair = lax.axis_index("depth") // 2
    modes = jnp.concatenate(
        [modes_ref[pl.ds(slot, PAIR_SIZE, stride=SLOTS), :] for slot in range(MODES)], 0
    )
    out_ref[...] = table_first(high_ref[pair], low_ref[pair], modes)


def final_kernel(parts_ref, numerator_ref, denominator_ref, out_ref):
    for half in range(2):
        lanes = slice(half * LANES, (half + 1) * LANES)
        filtered = (parts_ref[half] + parts_ref[half + 2]) + (
            parts_ref[half + 4] + parts_ref[half + 6]
        )
        out_ref[:, lanes] = (filtered + numerator_ref[:, lanes]) / denominator_ref[:, lanes]


def stencil_kernel(
    speed_hbm,
    memory_hbm,
    clamping_hbm,
    effect_a_hbm,
    effect_b_hbm,
    ambient_hbm,
    heat_hbm,
    fluid_hbm,
    memory_hbm_out,
    numerator_out,
    denominator_out,
    heat_out,
    fluid_out,
    speed_ref,
    memory_ref,
    clamping_ref,
    effect_a_ref,
    effect_b_ref,
    ambient_ref,
    memory_out,
    heat_in,
    fluid_in,
    heat_change,
    fluid_change,
    in_sem,
    out_sem,
    plane_sem,
):
    plane_loads = [
        pltpu.make_async_copy(source, target, plane_sem.at[at])
        for at, (source, target) in enumerate(
            (
                (speed_hbm, speed_ref),
                (memory_hbm, memory_ref),
                (clamping_hbm, clamping_ref),
                (effect_a_hbm, effect_a_ref),
                (effect_b_hbm, effect_b_ref),
                (ambient_hbm, ambient_ref),
            )
        )
    ]
    memory_store = pltpu.make_async_copy(memory_out, memory_hbm_out, plane_sem.at[6])
    for load in plane_loads:
        load.start()

    def pieces(source, target, sems, which):
        return [
            pltpu.make_async_copy(
                source.at[:, pl.ds(part * BLOCK, BLOCK), :],
                target.at[:, pl.ds(part * BLOCK, BLOCK), :],
                sems.at[which, part],
            )
            for part in range(ROWS // BLOCK)
        ]

    heat_loads = pieces(heat_hbm, heat_in, in_sem, 0)
    fluid_loads = pieces(fluid_hbm, fluid_in, in_sem, 1)
    heat_stores = pieces(heat_change, heat_out, out_sem, 0)
    fluid_stores = pieces(fluid_change, fluid_out, out_sem, 1)
    for part in range(ROWS // BLOCK):
        fluid_loads[part].start()
        heat_loads[part].start()
    for load in plane_loads:
        load.wait()
    for part in range(ROWS // BLOCK):
        fluid_loads[part].wait()
        heat_loads[part].wait()
        for row in range(part * BLOCK, (part + 1) * BLOCK, 8):
            rows = slice(row, row + 8)
            speed, memory = speed_ref[rows], memory_ref[rows]
            effect_a, effect_b = effect_a_ref[rows], effect_b_ref[rows]
            ratio = memory / effect_a
            argument = 0.5 * speed * jnp.exp(ratio)
            friction = effect_a * jnp.log(argument + jnp.sqrt(argument * argument + 1.0))
            root_term = jnp.sqrt(4.0 * jnp.exp(-2.0 * ratio) + speed * speed)
            effective = clamping_ref[rows] - fluid_in[0, rows]
            traction = effective * friction
            power = HEAT_GAIN * traction * speed
            memory_change = effect_b * (jnp.exp((REF_FRICTION - memory) / effect_b) - speed)
            memory_out[rows] = memory_change
            heat, fluid = heat_in[0, rows], fluid_in[0, rows]
            heat_above, fluid_above = heat_in[1, rows], fluid_in[1, rows]
            heat_below, fluid_below = heat_above, fluid_above
            for point in range(POINTS):
                bent = heat_below - 2.0 * heat
                pressed = fluid_below - 2.0 * fluid
                if point + 1 < POINTS:
                    bent = bent + heat_above
                    pressed = pressed + fluid_above
                warmed = HEAT_DIFFUSIVITY * bent + math.exp(-((point / HEAT_WIDTH) ** 2)) * power
                pressed = FLUID_DIFFUSIVITY * pressed + FLUID_TOGGLE * warmed
                heat_change[point, rows] = warmed
                fluid_change[point, rows] = pressed
                if point == 0:
                    extra = (
                        friction * pressed - effective * (speed / root_term) * memory_change
                    )
                    numerator_out[rows] = extra + RELAXATION * (
                        ambient_ref[rows] - DAMPING * speed - traction
                    )
                    denominator_out[rows] = effective * effect_a / root_term + DAMPING
                heat_below, fluid_below = heat, fluid
                heat, fluid = heat_above, fluid_above
                if point + 2 < POINTS:
                    heat_above, fluid_above = heat_in[point + 2, rows], fluid_in[point + 2, rows]
        heat_stores[part].start()
        fluid_stores[part].start()
    memory_store.start()
    memory_store.wait()
    for part in range(ROWS // BLOCK):
        heat_stores[part].wait()
        fluid_stores[part].wait()


def whole(count):
    return [pl.BlockSpec(memory_space=pltpu.VMEM)] * count


def anywhere(count):
    return [pl.BlockSpec(memory_space=pltpu.HBM)] * count


def in_hbm(*arrays):
    return [pltpu.with_memory_space_constraint(jnp.asarray(x), pltpu.HBM) for x in arrays]


def cost(flops, moved):
    return pl.CostEstimate(flops=flops, bytes_accessed=moved, transcendentals=0)


def shape(*dims):
    return jax.ShapeDtypeStruct(dims, F32)


BLOCK = 16


def grant(mebibytes):
    return pltpu.CompilerParams(vmem_limit_bytes=mebibytes * 1024 * 1024)


def shards(
    sliding_speed,
    offset_displacement,
    contact_memory,
    clamping_traction,
    instant_effect_a,
    healing_effect_b,
    ambient_traction,
    heat_level,
    fluid_load,
):
    depth_forward, depth_inverse = depth_tables()
    coarse_forward, coarse_inverse = coarse_tables()
    fine_forward, fine_inverse = fine_tables()
    small = ROWS * COLS * 4
    groups = [
        [(2 * pair + half) * STRIKE_PARTS + part for part in range(STRIKE_PARTS) for half in (0, 1)]
        for pair in range(PAIRS)
    ]

    def over_depth(pieces):
        return lax.all_to_all(pieces, "depth", split_axis=0, concat_axis=0)

    def over_pair(pieces):
        pieces = pieces.reshape(PAIR_SIZE, SLOTS, LANES)
        moved = lax.all_to_all(
            pieces, ("depth", "strike"), split_axis=0, concat_axis=0, axis_index_groups=groups
        )
        return moved.reshape(PAIR_SIZE * SLOTS, LANES)

    sent, depth_high, depth_low = pl.pallas_call(
        field_kernel,
        out_shape=(
            shape(DEPTH_PARTS, ROWS, LANES),
            pltpu.VMEM((PAIR_MODES, DEPTH), BF16),
            pltpu.VMEM((PAIR_MODES, DEPTH), BF16),
        ),
        in_specs=[pl.BlockSpec(memory_space=pltpu.HBM)] * 4,
        out_specs=whole(3),
        scratch_shapes=[pltpu.VMEM((ROWS, COLS), F32)] * 2 + [pltpu.SemaphoreType.DMA((4,))],
        compiler_params=grant(4),
        cost_estimate=cost(2 * ROWS * COLS, 12 * small),
    )(*in_hbm(sliding_speed, offset_displacement, *halves(depth_forward)))
    columns = over_depth(sent)

    modes = pl.pallas_call(
        depth_kernel,
        out_shape=shape(PAIR_SIZE * SLOTS, LANES),
        in_specs=whole(3),
        out_specs=pl.BlockSpec(memory_space=pltpu.VMEM),
        compiler_params=grant(10),
        cost_estimate=cost(6 * PAIR_MODES * DEPTH * LANES, 12 * small),
    )(columns.reshape(DEPTH, LANES), depth_high, depth_low)

    filtered = pl.pallas_call(
        strike_kernel,
        out_shape=shape(PAIR_SIZE * SLOTS, LANES),
        in_specs=whole(13),
        out_specs=pl.BlockSpec(memory_space=pltpu.VMEM),
        compiler_params=grant(6),
        cost_estimate=cost(6 * 4 * 256 * 256 * LANES, 15 * small),
    )(
        over_pair(modes),
        *halves(coarse_forward),
        *halves(fine_forward),
        *halves(fine_inverse),
        *halves(coarse_inverse),
        *class_tables(),
    )

    sent = pl.pallas_call(
        depth_back_kernel,
        out_shape=shape(DEPTH, LANES),
        in_specs=whole(3),
        out_specs=pl.BlockSpec(memory_space=pltpu.VMEM),
        compiler_params=grant(10),
        cost_estimate=cost(6 * PAIR_MODES * DEPTH * LANES, 12 * small),
    )(over_pair(filtered), *halves(depth_inverse))
    parts = over_depth(sent.reshape(DEPTH_PARTS, ROWS, LANES))

    memory_change, numerator, denominator, heat_level_change, fluid_load_change = pl.pallas_call(
        stencil_kernel,
        out_shape=(
            shape(ROWS, COLS),
            pltpu.VMEM((ROWS, COLS), F32),
            pltpu.VMEM((ROWS, COLS), F32),
            shape(POINTS, ROWS, COLS),
            shape(POINTS, ROWS, COLS),
        ),
        in_specs=anywhere(8),
        out_specs=anywhere(1) + whole(2) + anywhere(2),
        scratch_shapes=[pltpu.VMEM((ROWS, COLS), F32)] * 7
        + [pltpu.VMEM((POINTS, ROWS, COLS), F32)] * 4
        + [pltpu.SemaphoreType.DMA((2, ROWS // BLOCK))] * 2
        + [pltpu.SemaphoreType.DMA((7,))],
        compiler_params=grant(20),
        cost_estimate=cost(18 * POINTS * ROWS * COLS, 137 * small),
    )(
        *in_hbm(
            sliding_speed,
            contact_memory,
            clamping_traction,
            instant_effect_a,
            healing_effect_b,
            ambient_traction,
            heat_level,
            fluid_load,
        )
    )

    sliding_acceleration = pl.pallas_call(
        final_kernel,
        out_shape=shape(ROWS, COLS),
        in_specs=whole(3),
        out_specs=pl.BlockSpec(memory_space=pltpu.VMEM),
        compiler_params=grant(4),
        cost_estimate=cost(5 * ROWS * COLS, 7 * small),
    )(parts, numerator, denominator)
    return (sliding_acceleration, memory_change, heat_level_change, fluid_load_change)


def solution(mesh):
    plane = P("depth", "strike")
    block = P(None, "depth", "strike")
    return jax.shard_map(
        shards,
        mesh=mesh,
        in_specs=(plane,) * 7 + (block,) * 2,
        out_specs=(plane, plane, block, block),
        check_vma=False,
    )
```

time: 86.5 us -> 70.5 us (0.82); the launches traced: 84.9 us -> 70.2 us
  blocking collectives: 15 us -> 52.5 us
  starting transfers between devices: 23.2 us -> 3.96 us
  waiting for transfers between devices: 18.7 us -> 2.36 us
  Pallas kernels: 21.3 us -> 10.5 us
  local copies, waits for them, and re-layouts: 5.08 us -> 0.1 us
  other arithmetic: 0.96 us -> 0 us
    all_to_all x1 -> x3, blocking collectives: 15 us -> 52.5 us  [the longest x2 36.4 us: over_pair(): lax.all_to_all(pieces, ('depth', 'strike'), split_axis=0, concat_axis=0,...]
    all_to_all x3 -> x1, starting transfers between devices: 23.2 us -> 3.96 us  [over_depth(): return lax.all_to_all(pieces, 'depth', split_axis=0, concat_axis=0)]
    all_to_all x3 -> x1, waiting for transfers between devices: 18.7 us -> 2.36 us  [over_depth(): return lax.all_to_all(pieces, 'depth', split_axis=0, concat_axis=0)]
    pallas_call x5, Pallas kernels: 19 us -> 9.78 us  [the longest x1 5.88 us: shards(): pl.pallas_call(stencil_kernel, out_shape=(shape(ROWS, COLS), pltpu.VMEM((...]
    unnamed x6 -> x28, local copies, waits for them, and re-layouts: 2.41 us -> 0.1 us
    dynamic_slice x1 -> x0, local copies, waits for them, and re-layouts: 1.72 us -> none  [shards(): lax.dynamic_slice_in_dim(jnp.asarray(table), depth_pos * ROWS, ROWS, 0)]
    pallas_call x1, Pallas kernels: 2.27 us -> 0.67 us  [shards(): pl.pallas_call(final_kernel, out_shape=shape(ROWS, COLS), in_specs=whole(...]
    add x1 -> x0, other arithmetic: 0.96 us -> none  [shards(): field = sliding_speed + RELAXATION * offset_displacement]
  transfers between devices with their start and end apart: 3 -> 1, of which waited for: 2 -> 1; matrix products, arithmetic and copies ran while one was open for 2% -> 0% of each run, Pallas kernels for 14% -> 8%
where the time goes in v2:
time: 70.5 us; the launch traced here: 70.2 us
  blocking collectives  52.5 us (74%)
  Pallas kernels  10.5 us (15%)
  starting transfers between devices  3.96 us (6%)
  waiting for transfers between devices  2.36 us (3%)
  between operations  0.84 us (1%)
    all_to_all x2, blocking collectives, over_pair(): lax.all_to_all(pieces, ('depth', 'strike'), split_axis=0, concat_axis=0,...  36.4 us
    all_to_all x1, blocking collectives, over_depth(): return lax.all_to_all(pieces, 'depth', split_axis=0, concat_axis=0)  16 us
    pallas_call x1, Pallas kernels, shards(): pl.pallas_call(stencil_kernel, out_shape=(shape(ROWS, COLS), pltpu.VMEM((...  5.88 us
    all_to_all x1, starting transfers between devices, over_depth(): return lax.all_to_all(pieces, 'depth', split_axis=0, concat_axis=0)  3.96 us
    all_to_all x1, waiting for transfers between devices, over_depth(): return lax.all_to_all(pieces, 'depth', split_axis=0, concat_axis=0)  2.36 us
  transfers between devices with their start and end apart: 1, of which 1 were waited for; matrix products, arithmetic and copies ran while one was open for 0% of the time, Pallas kernels for 8%

profile of v2, /device:TPU:1, one launch (start us, length us, event | category | flops | bytes accessed | tf_op | source)
XLA Modules:
  0.0 70.2 jit_solution(7650283091685623365)
XLA Ops:
  0.6 0.0 copy-start.10
  0.6 0.0 copy-start.11
  0.7 0.0 copy-start.12
  0.7 0.0 copy-start.13
  0.7 0.0 copy-start.2
  0.7 0.0 copy-start.3
  0.7 0.0 copy-start.4
  0.7 0.0 copy-start.5
  0.7 0.0 copy-start.6
  0.7 0.0 copy-start.7
  0.8 0.0 copy-start.8
  0.8 0.0 copy-start.9
  0.8 0.0 copy-start
  0.8 0.0 copy-start.1
  0.8 1.4 %shard_map.264 = (f32[8,96,128]{2,1,0:T(8,128)S(1)}, bf16[192,768]{1,0:T(8,128)(2,1)S(1)}, bf16[192,768]{1,0:T(8,128)(2,1)S(1)}) custom-call(f32[96,256]{1,0:T(8,128)} %speed_hbm.3, f32[96,256]{1,0:T(8,128)} %slip_hbm.1, bf16[4,192,768]{2,1,0:T(8,128)(2,1)} %constant.32.clone.table_high, bf16[4,192,768]{2,1,0:T(8,128)(2,1)} %constant.33.clone.table_low), custom_call_target="tpu_custom_call" | custom-call | flops 49152 | bytes 1179648 | tf_op jit(solution)/shard_map/pallas_call | solution.py:395
  2.2 16.0 %all_to_all.20 = f32[8,96,128]{2,1,0:T(8,128)S(1)} all-to-all(f32[8,96,128]{2,1,0:T(8,128)S(1)} %get-tuple-element.12), channel_id=1, replica_groups=mesh['strike'=32,'depth'=8] {'depth'}, dimensions={0} | all-to-all | bytes 786432 | tf_op jit(solution)/shard_map/all_to_all | solution.py:386
  18.2 0.4 shard_map.265
  18.6 22.0 %all_to_all.21 = f32[64,4,128]{2,1,0:T(4,128)S(1)} all-to-all(f32[64,4,128]{2,1,0:T(4,128)S(1)} %bitcast.9), channel_id=1, replica_groups={{0,1,8,9,16,17,24,25,32,33,40,41,48,49,56,57,64,65,72,73,80,81,88,89,96..., dimensions={0} | all-to-all | bytes 262144 | tf_op jit(solution)/shard_map/all_to_all | solution.py:390
  40.6 0.0 copy-done.10
  40.6 0.0 copy-done.11
  40.6 0.0 copy-done.12
  40.7 0.0 copy-done.13
  40.7 0.0 copy-done.2
  40.7 0.0 copy-done.3
  40.7 0.0 copy-done.4
  40.7 0.9 %shard_map.266 = f32[256,128]{1,0:T(8,128)S(1)} custom-call(f32[256,128]{1,0:T(8,128)S(1)} %bitcast.7, bf16[224,256]{1,0:T(8,128)(2,1)S(1)} %copy-done.9, bf16[224,256]{1,0:T(8,128)(2,1)S(1)} %copy-done.8, bf16[256,256]{1,0:T(8,128)(2,1)S(1)} %copy-done.7, bf16[256,256]{1,0:T(8,128)(2,1)S(1)} %copy-done.6, bf16[256,256]{1,0:T(8,128)(2,1)S(1)} %copy-done.5, ...), custom_call_target="tpu_custom_call" | custom-call | flops 201326592 | bytes 1474560 | tf_op jit(solution)/shard_map/pallas_call | solution.py:419
  41.7 14.4 %all_to_all.22 = f32[64,4,128]{2,1,0:T(4,128)S(1)} all-to-all(f32[64,4,128]{2,1,0:T(4,128)S(1)} %bitcast.8), channel_id=1, replica_groups={{0,1,8,9,16,17,24,25,32,33,40,41,48,49,56,57,64,65,72,73,80,81,88,89,96..., dimensions={0} | all-to-all | bytes 262144 | tf_op jit(solution)/shard_map/all_to_all | solution.py:390
  56.1 1.2 %shard_map.267 = f32[768,128]{1,0:T(8,128)} custom-call(f32[256,128]{1,0:T(8,128)S(1)} %bitcast.10, bf16[4,768,192]{2,1,0:T(8,128)(2,1)S(1)} %copy-done.1, bf16[4,768,192]{2,1,0:T(8,128)(2,1)S(1)} %copy-done), custom_call_target="tpu_custom_call" | custom-call | flops 113246208 | bytes 1179648 | tf_op jit(solution)/shard_map/pallas_call | solution.py:435
  57.3 4.0 %all-to-all-start.3 = ((f32[8,96,128]{2,1,0:T(8,128)}), f32[8,96,128]{2,1,0:T(8,128)S(1)}, u32[]{:S(2)}, u32[]{:S(2)}) async-start(f32[8,96,128]{2,1,0:T(8,128)} %bitcast.5), calls=%async_computation.3 | async-start | bytes 786432 | tf_op jit(solution)/shard_map/all_to_all | solution.py:386
  61.3 5.9 %shard_map.268 = (f32[96,256]{1,0:T(8,128)}, f32[96,256]{1,0:T(8,128)S(1)}, f32[96,256]{1,0:T(8,128)S(1)}, f32[32,96,256]{2,1,0:T(8,128)}, f32[32,96,256]{2,1,0:T(8,128)}) custom-call(f32[96,256]{1,0:T(8,128)} %speed_hbm.3, f32[96,256]{1,0:T(8,128)} %memory_hbm.1, f32[96,256]{1,0:T(8,128)} %clamping_hbm.1, f32[96,256]{1,0:T(8,128)} %effect_a_hbm.1, ...), custom_call_target="tpu_custom_call" | custom-call | flops 14155776 | bytes 13467648 | tf_op jit(solution)/shard_map/pallas_call | solution.py:445
  67.2 2.4 %all-to-all-done.3.parts_ref = f32[8,96,128]{2,1,0:T(8,128)S(1)} async-done(((f32[8,96,128]{2,1,0:T(8,128)}), f32[8,96,128]{2,1,0:T(8,128)S(1)}, u32[]{:S(2)}, u32[]{:S(2)}) %all-to-all-start.3) | async-done | bytes 393248 | tf_op jit(solution)/shard_map/all_to_all | solution.py:386
  69.5 0.7 shard_map.269
  (7 shorter events, 0.0 us)
Async XLA Ops:
  0.6 40.0 %copy-start.10 = (f32[112,128]{1,0:T(8,128)S(1)}, f32[112,128]{1,0:T(8,128)}, u32[]{:S(2)}) copy-start(f32[112,128]{1,0:T(8,128)} %constant.45.clone.offset_ref) | copy-start | bytes 172036
  0.6 40.0 %copy-start.11 = (f32[112,128]{1,0:T(8,128)S(1)}, f32[112,128]{1,0:T(8,128)}, u32[]{:S(2)}) copy-start(f32[112,128]{1,0:T(8,128)} %constant.44.clone.strike_square_ref) | copy-start | bytes 172036
  0.7 40.0 %copy-start.12 = (f32[112,128]{1,0:T(8,128)S(1)}, f32[112,128]{1,0:T(8,128)}, u32[]{:S(2)}) copy-start(f32[112,128]{1,0:T(8,128)} %constant.43.clone.sin_ref) | copy-start | bytes 172036
  0.7 40.0 %copy-start.13 = (f32[112,128]{1,0:T(8,128)S(1)}, f32[112,128]{1,0:T(8,128)}, u32[]{:S(2)}) copy-start(f32[112,128]{1,0:T(8,128)} %constant.42.clone.cos_ref) | copy-start | bytes 172036
  0.7 40.0 %copy-start.2 = (bf16[256,224]{1,0:T(8,128)(2,1)S(1)}, bf16[256,224]{1,0:T(8,128)(2,1)}, u32[]{:S(2)}) copy-start(bf16[256,224]{1,0:T(8,128)(2,1)} %constant.41.clone.out_low) | copy-start | bytes 344068
  0.7 40.0 %copy-start.3 = (bf16[256,224]{1,0:T(8,128)(2,1)S(1)}, bf16[256,224]{1,0:T(8,128)(2,1)}, u32[]{:S(2)}) copy-start(bf16[256,224]{1,0:T(8,128)(2,1)} %constant.40.clone.out_high) | copy-start | bytes 344068
  0.7 40.0 %copy-start.4 = (bf16[256,256]{1,0:T(8,128)(2,1)S(1)}, bf16[256,256]{1,0:T(8,128)(2,1)}, u32[]{:S(2)}) copy-start(bf16[256,256]{1,0:T(8,128)(2,1)} %constant.39.clone.back_low) | copy-start | bytes 393220
  0.7 40.0 %copy-start.5 = (bf16[256,256]{1,0:T(8,128)(2,1)S(1)}, bf16[256,256]{1,0:T(8,128)(2,1)}, u32[]{:S(2)}) copy-start(bf16[256,256]{1,0:T(8,128)(2,1)} %constant.38.clone.back_high) | copy-start | bytes 393220
  0.7 40.0 %copy-start.6 = (bf16[256,256]{1,0:T(8,128)(2,1)S(1)}, bf16[256,256]{1,0:T(8,128)(2,1)}, u32[]{:S(2)}) copy-start(bf16[256,256]{1,0:T(8,128)(2,1)} %constant.37.clone.fine_low) | copy-start | bytes 393220
  0.7 40.0 %copy-start.7 = (bf16[256,256]{1,0:T(8,128)(2,1)S(1)}, bf16[256,256]{1,0:T(8,128)(2,1)}, u32[]{:S(2)}) copy-start(bf16[256,256]{1,0:T(8,128)(2,1)} %constant.36.clone.fine_high) | copy-start | bytes 393220
  0.8 40.0 %copy-start.8 = (bf16[224,256]{1,0:T(8,128)(2,1)S(1)}, bf16[224,256]{1,0:T(8,128)(2,1)}, u32[]{:S(2)}) copy-start(bf16[224,256]{1,0:T(8,128)(2,1)} %constant.35.clone.coarse_low) | copy-start | bytes 344068
  0.8 40.0 %copy-start.9 = (bf16[224,256]{1,0:T(8,128)(2,1)S(1)}, bf16[224,256]{1,0:T(8,128)(2,1)}, u32[]{:S(2)}) copy-start(bf16[224,256]{1,0:T(8,128)(2,1)} %constant.34.clone.coarse_high) | copy-start | bytes 344068
  0.8 55.3 %copy-start = (bf16[4,768,192]{2,1,0:T(8,128)(2,1)S(1)}, bf16[4,768,192]{2,1,0:T(8,128)(2,1)}, u32[]{:S(2)}) copy-start(bf16[4,768,192]{2,1,0:T(8,128)(2,1)} %constant.47.clone.low_ref) | copy-start | bytes 3538948
  0.8 55.3 %copy-start.1 = (bf16[4,768,192]{2,1,0:T(8,128)(2,1)S(1)}, bf16[4,768,192]{2,1,0:T(8,128)(2,1)}, u32[]{:S(2)}) copy-start(bf16[4,768,192]{2,1,0:T(8,128)(2,1)} %constant.46.clone.high_ref) | copy-start | bytes 3538948
  57.3 12.2 %all-to-all-start.3 = ((f32[8,96,128]{2,1,0:T(8,128)}), f32[8,96,128]{2,1,0:T(8,128)S(1)}, u32[]{:S(2)}, u32[]{:S(2)}) async-start(f32[8,96,128]{2,1,0:T(8,128)} %bitcast.5), calls=%async_computation.3 | async-start | bytes 786432 | tf_op jit(solution)/shard_map/all_to_all | solution.py:386

commit v3 on v2

--- a/solution.py
+++ b/solution.py
@@ -33,7 +33,7 @@
 PAIR_MODES = DEPTH // PAIRS
 PAIR_SIZE = 2 * STRIKE_PARTS
 MODES = 3
-SLOTS = 4
+PAIR_ROWS = PAIR_SIZE * MODES
 SPEC_ROWS = 112
 
 F32 = jnp.float32
@@ -61,8 +61,8 @@
 
 def coarse_tables():
     angle = 2.0 * np.pi / COARSE * (np.arange(CLASSES)[:, None] * np.arange(COARSE)[None, :] % COARSE)
-    forward = np.zeros((2, SPEC_ROWS, COARSE, SLOTS))
-    inverse = np.zeros((COARSE, SLOTS, 2, SPEC_ROWS))
+    forward = np.zeros((2, SPEC_ROWS, COARSE, MODES))
+    inverse = np.zeros((COARSE, MODES, 2, SPEC_ROWS))
     weight = np.where(np.arange(CLASSES) % (COARSE // 2) == 0, 1.0, 2.0)[:, None]
     for mode in range(MODES):
         at = np.arange(CLASSES) * MODES + mode
@@ -70,9 +70,11 @@
         forward[1, at, :, mode] = -np.sin(angle)
         inverse[:, mode, 0, at] = (weight * np.cos(angle)).T
         inverse[:, mode, 1, at] = (-weight * np.sin(angle)).T
+    piece = np.arange(PAIR_SIZE)
+    order = 2 * (piece % STRIKE_PARTS) + piece // STRIKE_PARTS
     return (
-        forward.reshape(2 * SPEC_ROWS, COARSE * SLOTS),
-        inverse.reshape(COARSE * SLOTS, 2 * SPEC_ROWS),
+        forward[:, :, order].reshape(2 * SPEC_ROWS, PAIR_ROWS),
+        inverse[order].reshape(PAIR_ROWS, 2 * SPEC_ROWS),
     )
 
 
@@ -156,11 +158,10 @@
 
 def depth_kernel(fields_ref, high_ref, low_ref, out_ref):
     modes = table_first(high_ref[...], low_ref[...], fields_ref[...])
-    for slot in range(SLOTS):
-        piece = jnp.zeros((PAIR_SIZE, LANES), F32)
-        if slot < MODES:
-            piece = modes[slot * PAIR_SIZE : (slot + 1) * PAIR_SIZE]
-        out_ref[pl.ds(slot, PAIR_SIZE, stride=SLOTS), :] = piece
+    for slot in range(MODES):
+        out_ref[pl.ds(slot, PAIR_SIZE, stride=MODES), :] = modes[
+            slot * PAIR_SIZE : (slot + 1) * PAIR_SIZE
+        ]
 
 
 def strike_kernel(
@@ -181,7 +182,9 @@
 ):
     cosine, sine = cos_ref[...], sin_ref[...]
     depth_pos = lax.axis_index("depth")
-    base = depth_pos // 2 * PAIR_MODES + 2 * lax.axis_index("strike") + depth_pos % 2
+    base = (
+        depth_pos // 2 * PAIR_MODES + depth_pos % 2 * STRIKE_PARTS + lax.axis_index("strike")
+    )
     depth_index = offset_ref[...] + base.astype(F32)
     depth_wave = 2.0 * math.pi / DEPTH * jnp.minimum(depth_index, DEPTH - depth_index)
     depth_square = depth_wave * depth_wave
@@ -206,7 +209,7 @@
 def depth_back_kernel(modes_ref, high_ref, low_ref, out_ref):
     pair = lax.axis_index("depth") // 2
     modes = jnp.concatenate(
-        [modes_ref[pl.ds(slot, PAIR_SIZE, stride=SLOTS), :] for slot in range(MODES)], 0
+        [modes_ref[pl.ds(slot, PAIR_SIZE, stride=MODES), :] for slot in range(MODES)], 0
     )
     out_ref[...] = table_first(high_ref[pair], low_ref[pair], modes)
 
@@ -378,7 +381,7 @@
     fine_forward, fine_inverse = fine_tables()
     small = ROWS * COLS * 4
     groups = [
-        [(2 * pair + half) * STRIKE_PARTS + part for part in range(STRIKE_PARTS) for half in (0, 1)]
+        [(2 * pair + half) * STRIKE_PARTS + part for half in (0, 1) for part in range(STRIKE_PARTS)]
         for pair in range(PAIRS)
     ]
 
@@ -386,11 +389,11 @@
         return lax.all_to_all(pieces, "depth", split_axis=0, concat_axis=0)
 
     def over_pair(pieces):
-        pieces = pieces.reshape(PAIR_SIZE, SLOTS, LANES)
+        pieces = pieces.reshape(PAIR_SIZE, 1, MODES * LANES)
         moved = lax.all_to_all(
             pieces, ("depth", "strike"), split_axis=0, concat_axis=0, axis_index_groups=groups
         )
-        return moved.reshape(PAIR_SIZE * SLOTS, LANES)
+        return moved.reshape(PAIR_ROWS, LANES)
 
     sent, depth_high, depth_low = pl.pallas_call(
         field_kernel,
@@ -409,7 +412,7 @@
 
     modes = pl.pallas_call(
         depth_kernel,
-        out_shape=shape(PAIR_SIZE * SLOTS, LANES),
+        out_shape=shape(PAIR_ROWS, LANES),
         in_specs=whole(3),
         out_specs=pl.BlockSpec(memory_space=pltpu.VMEM),
         compiler_params=grant(10),
@@ -418,7 +421,7 @@
 
     filtered = pl.pallas_call(
         strike_kernel,
-        out_shape=shape(PAIR_SIZE * SLOTS, LANES),
+        out_shape=shape(PAIR_ROWS, LANES),
         in_specs=whole(13),
         out_specs=pl.BlockSpec(memory_space=pltpu.VMEM),
         compiler_params=grant(6),

time: 70.5 us -> 67.9 us (0.963)
  blocking collectives: 52.5 us -> 49.7 us
    all_to_all x2, blocking collectives: 36.4 us -> 33.7 us  [over_pair(): lax.all_to_all(pieces, ('depth', 'strike'), split_axis=0, concat_axis=0,...]
  transfers between devices with their start and end apart: 1 -> 1, of which waited for: 1 -> 1; matrix products, arithmetic and copies ran while one was open for 0% -> 0% of each run, Pallas kernels for 8% -> 9%
where the time goes in v3:
time: 67.9 us; the launch traced here: 67.4 us
  blocking collectives  49.7 us (73%)
  Pallas kernels  10.4 us (15%)
  starting transfers between devices  3.95 us (6%)
  waiting for transfers between devices  2.35 us (3%)
  between operations  0.85 us (1%)
    all_to_all x2, blocking collectives, over_pair(): lax.all_to_all(pieces, ('depth', 'strike'), split_axis=0, concat_axis=0,...  33.7 us
    all_to_all x1, blocking collectives, over_depth(): return lax.all_to_all(pieces, 'depth', split_axis=0, concat_axis=0)  16 us
    pallas_call x1, Pallas kernels, shards(): pl.pallas_call(stencil_kernel, out_shape=(shape(ROWS, COLS), pltpu.VMEM((...  5.88 us
    all_to_all x1, starting transfers between devices, over_depth(): return lax.all_to_all(pieces, 'depth', split_axis=0, concat_axis=0)  3.95 us
    all_to_all x1, waiting for transfers between devices, over_depth(): return lax.all_to_all(pieces, 'depth', split_axis=0, concat_axis=0)  2.35 us
    pallas_call x1, Pallas kernels, shards(): pl.pallas_call(field_kernel, out_shape=(shape(DEPTH_PARTS, ROWS, LANES),...  1.36 us
  transfers between devices with their start and end apart: 1, of which 1 were waited for; matrix products, arithmetic and copies ran while one was open for 0% of the time, Pallas kernels for 9%

profile of v3, /device:TPU:1, one launch (start us, length us, event | category | flops | bytes accessed | tf_op | source)
XLA Modules:
  0.0 67.4 jit_solution(10605386355859260002)
XLA Ops:
  0.6 0.0 copy-start.10
  0.6 0.0 copy-start.11
  0.7 0.0 copy-start.12
  0.7 0.0 copy-start.13
  0.7 0.0 copy-start.8
  0.7 0.0 copy-start.9
  0.7 0.0 copy-start.2
  0.7 0.0 copy-start.3
  0.7 0.0 copy-start.4
  0.7 0.0 copy-start.5
  0.8 0.0 copy-start.6
  0.8 0.0 copy-start.7
  0.8 0.0 copy-start
  0.8 0.0 copy-start.1
  0.8 1.4 %shard_map.264 = (f32[8,96,128]{2,1,0:T(8,128)S(1)}, bf16[192,768]{1,0:T(8,128)(2,1)S(1)}, bf16[192,768]{1,0:T(8,128)(2,1)S(1)}) custom-call(f32[96,256]{1,0:T(8,128)} %speed_hbm.3, f32[96,256]{1,0:T(8,128)} %slip_hbm.1, bf16[4,192,768]{2,1,0:T(8,128)(2,1)} %constant.32.clone.table_high, bf16[4,192,768]{2,1,0:T(8,128)(2,1)} %constant.33.clone.table_low), custom_call_target="tpu_custom_call" | custom-call | flops 49152 | bytes 1179648 | tf_op jit(solution)/shard_map/pallas_call | solution.py:398
  2.2 16.0 %all_to_all.20 = f32[8,96,128]{2,1,0:T(8,128)S(1)} all-to-all(f32[8,96,128]{2,1,0:T(8,128)S(1)} %get-tuple-element.12), channel_id=1, replica_groups=mesh['strike'=32,'depth'=8] {'depth'}, dimensions={0} | all-to-all | bytes 786432 | tf_op jit(solution)/shard_map/all_to_all | solution.py:389
  18.2 0.4 shard_map.265
  18.6 20.5 %all_to_all.21 = f32[64,1,384]{2,1,0:T(1,128)S(1)} all-to-all(f32[64,1,384]{2,1,0:T(1,128)S(1)} %bitcast.7), channel_id=1, replica_groups={{0,8,16,24,32,40,48,56,64,72,80,88,96,104,112,120,128,136,144,152,160,1..., dimensions={0} | all-to-all | bytes 196608 | tf_op jit(solution)/shard_map/all_to_all | solution.py:393
  39.1 0.0 copy-done.10
  39.1 0.0 copy-done.11
  39.1 0.0 copy-done.12
  39.1 0.0 copy-done.13
  39.1 0.0 copy-done.8
  39.2 0.0 copy-done.9
  39.2 0.9 %shard_map.266 = f32[192,128]{1,0:T(8,128)S(1)} custom-call(f32[192,128]{1,0:T(8,128)S(1)} %bitcast.8, bf16[224,192]{1,0:T(8,128)(2,1)S(1)} %copy-done.7, bf16[224,192]{1,0:T(8,128)(2,1)S(1)} %copy-done.6, bf16[256,256]{1,0:T(8,128)(2,1)S(1)} %copy-done.5, bf16[256,256]{1,0:T(8,128)(2,1)S(1)} %copy-done.4, bf16[256,256]{1,0:T(8,128)(2,1)S(1)} %copy-done.3, ...), custom_call_target="tpu_custom_call" | custom-call | flops 201326592 | bytes 1474560 | tf_op jit(solution)/shard_map/pallas_call | solution.py:422
  40.2 13.1 %all_to_all.22 = f32[64,1,384]{2,1,0:T(1,128)S(1)} all-to-all(f32[64,1,384]{2,1,0:T(1,128)S(1)} %bitcast.9), channel_id=1, replica_groups={{0,8,16,24,32,40,48,56,64,72,80,88,96,104,112,120,128,136,144,152,160,1..., dimensions={0} | all-to-all | bytes 196608 | tf_op jit(solution)/shard_map/all_to_all | solution.py:393
  53.3 0.0 copy-done.1
  53.3 1.2 %shard_map.267 = f32[768,128]{1,0:T(8,128)} custom-call(f32[192,128]{1,0:T(8,128)S(1)} %bitcast.10, bf16[4,768,192]{2,1,0:T(8,128)(2,1)S(1)} %copy-done.1, bf16[4,768,192]{2,1,0:T(8,128)(2,1)S(1)} %copy-done), custom_call_target="tpu_custom_call" | custom-call | flops 113246208 | bytes 1179648 | tf_op jit(solution)/shard_map/pallas_call | solution.py:438
  54.5 4.0 %all-to-all-start.3 = ((f32[8,96,128]{2,1,0:T(8,128)}), f32[8,96,128]{2,1,0:T(8,128)S(1)}, u32[]{:S(2)}, u32[]{:S(2)}) async-start(f32[8,96,128]{2,1,0:T(8,128)} %bitcast.5), calls=%async_computation.3 | async-start | bytes 786432 | tf_op jit(solution)/shard_map/all_to_all | solution.py:389
  58.5 5.9 %shard_map.268 = (f32[96,256]{1,0:T(8,128)}, f32[96,256]{1,0:T(8,128)S(1)}, f32[96,256]{1,0:T(8,128)S(1)}, f32[32,96,256]{2,1,0:T(8,128)}, f32[32,96,256]{2,1,0:T(8,128)}) custom-call(f32[96,256]{1,0:T(8,128)} %speed_hbm.3, f32[96,256]{1,0:T(8,128)} %memory_hbm.1, f32[96,256]{1,0:T(8,128)} %clamping_hbm.1, f32[96,256]{1,0:T(8,128)} %effect_a_hbm.1, ...), custom_call_target="tpu_custom_call" | custom-call | flops 14155776 | bytes 13467648 | tf_op jit(solution)/shard_map/pallas_call | solution.py:448
  64.4 2.4 %all-to-all-done.3.parts_ref = f32[8,96,128]{2,1,0:T(8,128)S(1)} async-done(((f32[8,96,128]{2,1,0:T(8,128)}), f32[8,96,128]{2,1,0:T(8,128)S(1)}, u32[]{:S(2)}, u32[]{:S(2)}) %all-to-all-start.3) | async-done | bytes 393248 | tf_op jit(solution)/shard_map/all_to_all | solution.py:389
  66.7 0.7 shard_map.269
  (7 shorter events, 0.0 us)
Async XLA Ops:
  0.6 38.5 %copy-start.10 = (f32[112,128]{1,0:T(8,128)S(1)}, f32[112,128]{1,0:T(8,128)}, u32[]{:S(2)}) copy-start(f32[112,128]{1,0:T(8,128)} %constant.45.clone.offset_ref) | copy-start | bytes 172036
  0.6 38.5 %copy-start.11 = (f32[112,128]{1,0:T(8,128)S(1)}, f32[112,128]{1,0:T(8,128)}, u32[]{:S(2)}) copy-start(f32[112,128]{1,0:T(8,128)} %constant.44.clone.strike_square_ref) | copy-start | bytes 172036
  0.7 38.5 %copy-start.12 = (f32[112,128]{1,0:T(8,128)S(1)}, f32[112,128]{1,0:T(8,128)}, u32[]{:S(2)}) copy-start(f32[112,128]{1,0:T(8,128)} %constant.43.clone.sin_ref) | copy-start | bytes 172036
  0.7 38.5 %copy-start.13 = (f32[112,128]{1,0:T(8,128)S(1)}, f32[112,128]{1,0:T(8,128)}, u32[]{:S(2)}) copy-start(f32[112,128]{1,0:T(8,128)} %constant.42.clone.cos_ref) | copy-start | bytes 172036
  0.7 38.5 %copy-start.8 = (bf16[192,224]{1,0:T(8,128)(2,1)S(1)}, bf16[192,224]{1,0:T(8,128)(2,1)}, u32[]{:S(2)}) copy-start(bf16[192,224]{1,0:T(8,128)(2,1)} %constant.41.clone.out_low) | copy-start | bytes 258052
  0.7 38.5 %copy-start.9 = (bf16[192,224]{1,0:T(8,128)(2,1)S(1)}, bf16[192,224]{1,0:T(8,128)(2,1)}, u32[]{:S(2)}) copy-start(bf16[192,224]{1,0:T(8,128)(2,1)} %constant.40.clone.out_high) | copy-start | bytes 258052
  0.7 38.5 %copy-start.2 = (bf16[256,256]{1,0:T(8,128)(2,1)S(1)}, bf16[256,256]{1,0:T(8,128)(2,1)}, u32[]{:S(2)}) copy-start(bf16[256,256]{1,0:T(8,128)(2,1)} %constant.39.clone.back_low) | copy-start | bytes 393220
  0.7 38.5 %copy-start.3 = (bf16[256,256]{1,0:T(8,128)(2,1)S(1)}, bf16[256,256]{1,0:T(8,128)(2,1)}, u32[]{:S(2)}) copy-start(bf16[256,256]{1,0:T(8,128)(2,1)} %constant.38.clone.back_high) | copy-start | bytes 393220
  0.7 38.5 %copy-start.4 = (bf16[256,256]{1,0:T(8,128)(2,1)S(1)}, bf16[256,256]{1,0:T(8,128)(2,1)}, u32[]{:S(2)}) copy-start(bf16[256,256]{1,0:T(8,128)(2,1)} %constant.37.clone.fine_low) | copy-start | bytes 393220
  0.7 38.5 %copy-start.5 = (bf16[256,256]{1,0:T(8,128)(2,1)S(1)}, bf16[256,256]{1,0:T(8,128)(2,1)}, u32[]{:S(2)}) copy-start(bf16[256,256]{1,0:T(8,128)(2,1)} %constant.36.clone.fine_high) | copy-start | bytes 393220
  0.8 38.5 %copy-start.6 = (bf16[224,192]{1,0:T(8,128)(2,1)S(1)}, bf16[224,192]{1,0:T(8,128)(2,1)}, u32[]{:S(2)}) copy-start(bf16[224,192]{1,0:T(8,128)(2,1)} %constant.35.clone.coarse_low) | copy-start | bytes 258052
  0.8 38.4 %copy-start.7 = (bf16[224,192]{1,0:T(8,128)(2,1)S(1)}, bf16[224,192]{1,0:T(8,128)(2,1)}, u32[]{:S(2)}) copy-start(bf16[224,192]{1,0:T(8,128)(2,1)} %constant.34.clone.coarse_high) | copy-start | bytes 258052
  0.8 52.5 %copy-start = (bf16[4,768,192]{2,1,0:T(8,128)(2,1)S(1)}, bf16[4,768,192]{2,1,0:T(8,128)(2,1)}, u32[]{:S(2)}) copy-start(bf16[4,768,192]{2,1,0:T(8,128)(2,1)} %constant.47.clone.low_ref) | copy-start | bytes 3538948
  0.8 52.5 %copy-start.1 = (bf16[4,768,192]{2,1,0:T(8,128)(2,1)S(1)}, bf16[4,768,192]{2,1,0:T(8,128)(2,1)}, u32[]{:S(2)}) copy-start(bf16[4,768,192]{2,1,0:T(8,128)(2,1)} %constant.46.clone.high_ref) | copy-start | bytes 3538948
  54.5 12.2 %all-to-all-start.3 = ((f32[8,96,128]{2,1,0:T(8,128)}), f32[8,96,128]{2,1,0:T(8,128)S(1)}, u32[]{:S(2)}, u32[]{:S(2)}) async-start(f32[8,96,128]{2,1,0:T(8,128)} %bitcast.5), calls=%async_computation.3 | async-start | bytes 786432 | tf_op jit(solution)/shard_map/all_to_all | solution.py:389

commit v4 on v3

--- a/solution.py
+++ b/solution.py
@@ -34,7 +34,17 @@
 PAIR_SIZE = 2 * STRIKE_PARTS
 MODES = 3
 PAIR_ROWS = PAIR_SIZE * MODES
+TABLE_CHUNKS = 1
+BACK_CHUNKS = 6
 SPEC_ROWS = 112
+
+ORDER = "hxzc"
+SIZES = {"h": 2, "x": 2, "z": 8, "c": 2}
+WEIGHTS = {name: math.prod(SIZES[k] for k in ORDER[at + 1 :]) for at, name in enumerate(ORDER)}
+DIGITS = [
+    {name: place // WEIGHTS[name] % SIZES[name] for name in ORDER} for place in range(PAIR_SIZE)
+]
+PIECES = [(16 * d["x"] + 2 * d["z"] + d["c"], d["h"]) for d in DIGITS]
 
 F32 = jnp.float32
 BF16 = jnp.bfloat16
@@ -43,20 +53,13 @@
 def halves(table):
     high = table.astype(ml_dtypes.bfloat16)
     low = (table - high.astype(np.float64)).astype(ml_dtypes.bfloat16)
-    return high, low
+    return np.concatenate([high, low], -2)
 
 
 def depth_table():
     index = np.arange(DEPTH)
     angle = 2.0 * np.pi / DEPTH * (index[:, None] * index[None, :] % DEPTH)
     return np.cos(angle) + np.sin(angle)
-
-
-def depth_tables():
-    table = depth_table()
-    forward = table.reshape(PAIRS, PAIR_MODES, DEPTH)
-    inverse = table.reshape(DEPTH, PAIRS, PAIR_MODES).transpose(1, 0, 2)
-    return forward, inverse
 
 
 def coarse_tables():
@@ -70,8 +73,7 @@
         forward[1, at, :, mode] = -np.sin(angle)
         inverse[:, mode, 0, at] = (weight * np.cos(angle)).T
         inverse[:, mode, 1, at] = (-weight * np.sin(angle)).T
-    piece = np.arange(PAIR_SIZE)
-    order = 2 * (piece % STRIKE_PARTS) + piece // STRIKE_PARTS
+    order = [2 * part + half for part, half in PIECES]
     return (
         forward[:, :, order].reshape(2 * SPEC_ROWS, PAIR_ROWS),
         inverse[order].reshape(PAIR_ROWS, 2 * SPEC_ROWS),
@@ -95,10 +97,8 @@
     wave = k_one[:, None] + COARSE * lane[None, :]
     strike_wave = 2.0 * np.pi / STRIKE * np.minimum(wave, STRIKE - wave)
     offset = np.broadcast_to((row % MODES * PAIR_SIZE)[:, None], (SPEC_ROWS, LANES))
-    return tuple(
-        np.asarray(table, np.float32)
-        for table in (np.cos(angle), np.sin(angle), strike_wave * strike_wave, offset)
-    )
+    tables = (np.cos(angle), np.sin(angle), strike_wave * strike_wave, offset)
+    return np.stack(tables).astype(np.float32)
 
 
 def split(values):
@@ -110,40 +110,48 @@
     return jnp.dot(left, right, preferred_element_type=F32)
 
 
-def table_first(high, low, values):
+def table_first(table, values):
+    rows = table.shape[0] // 2
     v_high, v_low = split(values)
-    return mm(high, v_high) + (mm(high, v_low) + mm(low, v_high))
-
-
-def table_last(values, high, low):
+    both = mm(table, v_high)
+    return both[:rows] + (both[rows:] + mm(table[:rows], v_low))
+
+
+def table_last(values, table):
+    rows, depth = values.shape
     v_high, v_low = split(values)
-    return mm(v_high, high) + (mm(v_low, high) + mm(v_high, low))
-
-
-def field_kernel(
-    speed_hbm,
-    slip_hbm,
-    table_high,
-    table_low,
-    out_ref,
-    high_out,
-    low_out,
-    speed_ref,
-    slip_ref,
-    sems,
-):
+    both = mm(jnp.concatenate([v_high, v_low], 0), table[:depth])
+    return both[:rows] + (both[rows:] + mm(v_high, table[depth:]))
+
+
+def table_turned(table, values):
+    rows = table.shape[0] // 2
+    v_high, v_low = split(values)
+
+    def product(left, right):
+        return lax.dot_general(
+            left, right, (((0,), (0,)), ((), ())), preferred_element_type=F32
+        )
+
+    return product(table[:rows], v_high) + (
+        product(table[:rows], v_low) + product(table[rows:], v_high)
+    )
+
+
+def field_kernel(speed_hbm, slip_hbm, table_hbm, out_ref, table_out, speed_ref, slip_ref, sems):
     pair = lax.axis_index("depth") // 2
     loads = [
         pltpu.make_async_copy(source, target, sems.at[at])
-        for at, (source, target) in enumerate(
-            (
-                (speed_hbm, speed_ref),
-                (slip_hbm, slip_ref),
-                (table_high.at[pair], high_out),
-                (table_low.at[pair], low_out),
+        for at, (source, target) in enumerate(((speed_hbm, speed_ref), (slip_hbm, slip_ref)))
+    ]
+    chunk = 2 * PAIR_MODES // TABLE_CHUNKS
+    for part in range(TABLE_CHUNKS):
+        rows = pl.ds(part * chunk, chunk)
+        loads.append(
+            pltpu.make_async_copy(
+                table_hbm.at[pair, rows], table_out.at[rows], sems.at[2 + part]
             )
         )
-    ]
     for load in loads:
         load.start()
     loads[0].wait()
@@ -152,66 +160,61 @@
     for part in range(DEPTH_PARTS):
         half = part % 2
         out_ref[part] = field[:, half * LANES : (half + 1) * LANES]
-    loads[2].wait()
-    loads[3].wait()
-
-
-def depth_kernel(fields_ref, high_ref, low_ref, out_ref):
-    modes = table_first(high_ref[...], low_ref[...], fields_ref[...])
+    for load in loads[2:]:
+        load.wait()
+
+
+def depth_kernel(fields_ref, table_ref, out_ref):
+    modes = table_first(table_ref[...], fields_ref[...])
     for slot in range(MODES):
         out_ref[pl.ds(slot, PAIR_SIZE, stride=MODES), :] = modes[
             slot * PAIR_SIZE : (slot + 1) * PAIR_SIZE
         ]
 
 
-def strike_kernel(
-    modes_ref,
-    coarse_high,
-    coarse_low,
-    fine_high,
-    fine_low,
-    back_high,
-    back_low,
-    out_high,
-    out_low,
-    cos_ref,
-    sin_ref,
-    strike_square_ref,
-    offset_ref,
-    out_ref,
-):
-    cosine, sine = cos_ref[...], sin_ref[...]
-    depth_pos = lax.axis_index("depth")
-    base = (
-        depth_pos // 2 * PAIR_MODES + depth_pos % 2 * STRIKE_PARTS + lax.axis_index("strike")
-    )
-    depth_index = offset_ref[...] + base.astype(F32)
+def strike_kernel(modes_ref, coarse_ref, fine_ref, back_ref, out_table, class_ref, out_ref):
+    cosine, sine = class_ref[0], class_ref[1]
+    depth_pos, strike_pos = lax.axis_index("depth"), lax.axis_index("strike")
+    place = (
+        depth_pos % 2 * WEIGHTS["h"]
+        + strike_pos // 16 * WEIGHTS["x"]
+        + strike_pos // 2 % 8 * WEIGHTS["z"]
+        + strike_pos % 2 * WEIGHTS["c"]
+    )
+    base = depth_pos // 2 * PAIR_MODES + place
+    depth_index = class_ref[3] + base.astype(F32)
     depth_wave = 2.0 * math.pi / DEPTH * jnp.minimum(depth_index, DEPTH - depth_index)
     depth_square = depth_wave * depth_wave
-    strike_square = strike_square_ref[...]
+    strike_square = class_ref[2]
     wave_square = strike_square + depth_square
     kernel = (
         (-0.5 / (DEPTH * STRIKE))
         * (strike_square * ELASTIC + depth_square)
         / jnp.sqrt(jnp.where(wave_square > 0, wave_square, 1.0))
     )
-    coarse = table_first(coarse_high[...], coarse_low[...], modes_ref[...])
+    coarse = table_first(coarse_ref[...], modes_ref[...])
     real, imag = coarse[:SPEC_ROWS], coarse[SPEC_ROWS:]
     turned = jnp.concatenate([real * cosine + imag * sine, imag * cosine - real * sine], 1)
-    spectrum = table_last(turned, fine_high[...], fine_low[...])
+    spectrum = table_last(turned, fine_ref[...])
     spectrum = spectrum * jnp.concatenate([kernel, kernel], 1)
-    back = table_last(spectrum, back_high[...], back_low[...])
+    back = table_last(spectrum, back_ref[...])
     real, imag = back[:, :LANES], back[:, LANES:]
     turned = jnp.concatenate([real * cosine - imag * sine, imag * cosine + real * sine], 0)
-    out_ref[...] = table_first(out_high[...], out_low[...], turned)
-
-
-def depth_back_kernel(modes_ref, high_ref, low_ref, out_ref):
-    pair = lax.axis_index("depth") // 2
+    out_ref[...] = table_first(out_table[...], turned)
+
+
+def depth_back_kernel(modes_ref, table_ref, out_hbm, out_ref, sems):
     modes = jnp.concatenate(
         [modes_ref[pl.ds(slot, PAIR_SIZE, stride=MODES), :] for slot in range(MODES)], 0
     )
-    out_ref[...] = table_first(high_ref[pair], low_ref[pair], modes)
+    stores = []
+    for part in range(BACK_CHUNKS):
+        rows = slice(part * DEPTH // BACK_CHUNKS, (part + 1) * DEPTH // BACK_CHUNKS)
+        out_ref[rows] = table_turned(table_ref[:, rows], modes)
+        stores.append(pltpu.make_async_copy(out_ref.at[rows], out_hbm.at[rows], sems.at[part]))
+        stores[-1].start()
+    for store in stores:
+        store.wait()
 
 
 def final_kernel(parts_ref, numerator_ref, denominator_ref, out_ref):
@@ -376,13 +379,12 @@
     heat_level,
     fluid_load,
 ):
-    depth_forward, depth_inverse = depth_tables()
+    depth_forward = depth_table().reshape(PAIRS, PAIR_MODES, DEPTH)
     coarse_forward, coarse_inverse = coarse_tables()
     fine_forward, fine_inverse = fine_tables()
     small = ROWS * COLS * 4
     groups = [
-        [(2 * pair + half) * STRIKE_PARTS + part for half in (0, 1) for part in range(STRIKE_PARTS)]
-        for pair in range(PAIRS)
+        [(2 * pair + half) * STRIKE_PARTS + part for part, half in PIECES] for pair in range(PAIRS)
     ]
 
     def over_depth(pieces):
@@ -395,54 +397,55 @@
         )
         return moved.reshape(PAIR_ROWS, LANES)
 
-    sent, depth_high, depth_low = pl.pallas_call(
+    sent, depth_part = pl.pallas_call(
         field_kernel,
         out_shape=(
             shape(DEPTH_PARTS, ROWS, LANES),
-            pltpu.VMEM((PAIR_MODES, DEPTH), BF16),
-            pltpu.VMEM((PAIR_MODES, DEPTH), BF16),
+            pltpu.VMEM((2 * PAIR_MODES, DEPTH), BF16),
         ),
-        in_specs=[pl.BlockSpec(memory_space=pltpu.HBM)] * 4,
-        out_specs=whole(3),
-        scratch_shapes=[pltpu.VMEM((ROWS, COLS), F32)] * 2 + [pltpu.SemaphoreType.DMA((4,))],
+        in_specs=anywhere(3),
+        out_specs=whole(2),
+        scratch_shapes=[pltpu.VMEM((ROWS, COLS), F32)] * 2
+        + [pltpu.SemaphoreType.DMA((2 + TABLE_CHUNKS,))],
         compiler_params=grant(4),
         cost_estimate=cost(2 * ROWS * COLS, 12 * small),
-    )(*in_hbm(sliding_speed, offset_displacement, *halves(depth_forward)))
+    )(*in_hbm(sliding_speed, offset_displacement, halves(depth_forward)))
     columns = over_depth(sent)
 
     modes = pl.pallas_call(
         depth_kernel,
         out_shape=shape(PAIR_ROWS, LANES),
-        in_specs=whole(3),
+        in_specs=whole(2),
         out_specs=pl.BlockSpec(memory_space=pltpu.VMEM),
         compiler_params=grant(10),
         cost_estimate=cost(6 * PAIR_MODES * DEPTH * LANES, 12 * small),
-    )(columns.reshape(DEPTH, LANES), depth_high, depth_low)
+    )(columns.reshape(DEPTH, LANES), depth_part)
 
     filtered = pl.pallas_call(
         strike_kernel,
         out_shape=shape(PAIR_ROWS, LANES),
-        in_specs=whole(13),
+        in_specs=whole(6),
         out_specs=pl.BlockSpec(memory_space=pltpu.VMEM),
         compiler_params=grant(6),
         cost_estimate=cost(6 * 4 * 256 * 256 * LANES, 15 * small),
     )(
         over_pair(modes),
-        *halves(coarse_forward),
-        *halves(fine_forward),
-        *halves(fine_inverse),
-        *halves(coarse_inverse),
-        *class_tables(),
+        halves(coarse_forward),
+        halves(fine_forward),
+        halves(fine_inverse),
+        halves(coarse_inverse),
+        class_tables(),
     )
 
     sent = pl.pallas_call(
         depth_back_kernel,
         out_shape=shape(DEPTH, LANES),
-        in_specs=whole(3),
-        out_specs=pl.BlockSpec(memory_space=pltpu.VMEM),
+        in_specs=whole(2),
+        out_specs=pl.BlockSpec(memory_space=pltpu.HBM),
+        scratch_shapes=[pltpu.VMEM((DEPTH, LANES), F32), pltpu.SemaphoreType.DMA((BACK_CHUNKS,))],
         compiler_params=grant(10),
         cost_estimate=cost(6 * PAIR_MODES * DEPTH * LANES, 12 * small),
-    )(over_pair(filtered), *halves(depth_inverse))
+    )(over_pair(filtered), depth_part)
     parts = over_depth(sent.reshape(DEPTH_PARTS, ROWS, LANES))
 
     memory_change, numerator, denominator, heat_level_change, fluid_load_change = pl.pallas_call(

time: 67.9 us -> 67.5 us (level)
  no operation moved by 1% of the time
where the time goes in v4:
time: 67.5 us; the launch traced here: 67 us
  blocking collectives  49.6 us (73%)
  Pallas kernels  10.3 us (15%)
  starting transfers between devices  3.97 us (6%)
  waiting for transfers between devices  2.36 us (3%)
  between operations  0.73 us (1%)
    all_to_all x2, blocking collectives, over_pair(): lax.all_to_all(pieces, ('depth', 'strike'), split_axis=0, concat_axis=0,...  33.7 us
    all_to_all x1, blocking collectives, over_depth(): return lax.all_to_all(pieces, 'depth', split_axis=0, concat_axis=0)  15.9 us
    pallas_call x1, Pallas kernels, shards(): pl.pallas_call(stencil_kernel, out_shape=(shape(ROWS, COLS), pltpu.VMEM((...  5.88 us
    all_to_all x1, starting transfers between devices, over_depth(): return lax.all_to_all(pieces, 'depth', split_axis=0, concat_axis=0)  3.97 us
    all_to_all x1, waiting for transfers between devices, over_depth(): return lax.all_to_all(pieces, 'depth', split_axis=0, concat_axis=0)  2.36 us
  transfers between devices with their start and end apart: 1, of which 1 were waited for; matrix products, arithmetic and copies ran while one was open for 0% of the time, Pallas kernels for 9%

profile of v4, /device:TPU:1, one launch (start us, length us, event | category | flops | bytes accessed | tf_op | source)
XLA Modules:
  0.0 67.0 jit_solution(3280484858085704253)
XLA Ops:
  0.6 0.0 copy-start.2
  0.6 0.0 copy-start.4
  0.7 0.0 copy-start
  0.7 0.0 copy-start.1
  0.7 0.0 copy-start.3
  0.7 1.3 %shard_map.174 = (f32[8,96,128]{2,1,0:T(8,128)S(1)}, bf16[384,768]{1,0:T(8,128)(2,1)S(1)}) custom-call(f32[96,256]{1,0:T(8,128)} %speed_hbm.3, f32[96,256]{1,0:T(8,128)} %slip_hbm.1, bf16[4,384,768]{2,1,0:T(8,128)(2,1)} %constant.12.clone.table_hbm), custom_call_target="tpu_custom_call" | custom-call | flops 49152 | bytes 1179648 | tf_op jit(solution)/shard_map/pallas_call | solution.py:400
  2.0 15.9 %all_to_all.20 = f32[8,96,128]{2,1,0:T(8,128)S(1)} all-to-all(f32[8,96,128]{2,1,0:T(8,128)S(1)} %get-tuple-element.11), channel_id=1, replica_groups=mesh['strike'=32,'depth'=8] {'depth'}, dimensions={0} | all-to-all | bytes 786432 | tf_op jit(solution)/shard_map/all_to_all | solution.py:391
  17.9 0.4 shard_map.175
  18.3 20.5 %all_to_all.21 = f32[64,1,384]{2,1,0:T(1,128)S(1)} all-to-all(f32[64,1,384]{2,1,0:T(1,128)S(1)} %bitcast.8), channel_id=1, replica_groups={{0,8,16,24,32,40,48,56,64,72,80,88,96,104,112,120,128,136,144,152,160,1..., dimensions={0} | all-to-all | bytes 196608 | tf_op jit(solution)/shard_map/all_to_all | solution.py:395
  38.8 0.0 copy-done.2
  38.8 0.0 copy-done.4
  38.8 0.0 copy-done
  38.8 0.0 copy-done.1
  38.8 0.0 copy-done.3
  38.8 0.9 %shard_map.176 = f32[192,128]{1,0:T(8,128)S(1)} custom-call(f32[192,128]{1,0:T(8,128)S(1)} %bitcast.9, bf16[448,192]{1,0:T(8,128)(2,1)S(1)} %copy-done.3, bf16[512,256]{1,0:T(8,128)(2,1)S(1)} %copy-done.1, bf16[512,256]{1,0:T(8,128)(2,1)S(1)} %copy-done, bf16[384,224]{1,0:T(8,128)(2,1)S(1)} %copy-done.4, f32[4,112,128]{2,1,0:T(8,128)S(1)} %copy-done.2), custom_call_target="tpu_custom_call" | custom-call | flops 201326592 | bytes 1474560 | tf_op jit(solution)/shard_map/pallas_call | solution.py:424
  39.7 13.1 %all_to_all.22 = f32[64,1,384]{2,1,0:T(1,128)S(1)} all-to-all(f32[64,1,384]{2,1,0:T(1,128)S(1)} %bitcast.10), channel_id=1, replica_groups={{0,8,16,24,32,40,48,56,64,72,80,88,96,104,112,120,128,136,144,152,160,1..., dimensions={0} | all-to-all | bytes 196608 | tf_op jit(solution)/shard_map/all_to_all | solution.py:395
  52.9 1.2 %shard_map.177 = f32[768,128]{1,0:T(8,128)} custom-call(f32[192,128]{1,0:T(8,128)S(1)} %bitcast.7, bf16[384,768]{1,0:T(8,128)(2,1)S(1)} %get-tuple-element.12.table_ref), custom_call_target="tpu_custom_call" | custom-call | flops 113246208 | bytes 1179648 | tf_op jit(solution)/shard_map/pallas_call | solution.py:440
  54.1 4.0 %all-to-all-start.3 = ((f32[8,96,128]{2,1,0:T(8,128)}), f32[8,96,128]{2,1,0:T(8,128)S(1)}, u32[]{:S(2)}, u32[]{:S(2)}) async-start(f32[8,96,128]{2,1,0:T(8,128)} %bitcast.5), calls=%async_computation.3 | async-start | bytes 786432 | tf_op jit(solution)/shard_map/all_to_all | solution.py:391
  58.0 5.9 %shard_map.178 = (f32[96,256]{1,0:T(8,128)}, f32[96,256]{1,0:T(8,128)S(1)}, f32[96,256]{1,0:T(8,128)S(1)}, f32[32,96,256]{2,1,0:T(8,128)}, f32[32,96,256]{2,1,0:T(8,128)}) custom-call(f32[96,256]{1,0:T(8,128)} %speed_hbm.3, f32[96,256]{1,0:T(8,128)} %memory_hbm.1, f32[96,256]{1,0:T(8,128)} %clamping_hbm.1, f32[96,256]{1,0:T(8,128)} %effect_a_hbm.1, ...), custom_call_target="tpu_custom_call" | custom-call | flops 14155776 | bytes 13467648 | tf_op jit(solution)/shard_map/pallas_call | solution.py:451
  63.9 2.4 %all-to-all-done.3.parts_ref = f32[8,96,128]{2,1,0:T(8,128)S(1)} async-done(((f32[8,96,128]{2,1,0:T(8,128)}), f32[8,96,128]{2,1,0:T(8,128)S(1)}, u32[]{:S(2)}, u32[]{:S(2)}) %all-to-all-start.3) | async-done | bytes 393248 | tf_op jit(solution)/shard_map/all_to_all | solution.py:391
  66.3 0.7 %shard_map.179 = f32[96,256]{1,0:T(8,128)} custom-call(f32[8,96,128]{2,1,0:T(8,128)S(1)} %all-to-all-done.3.parts_ref, f32[96,256]{1,0:T(8,128)S(1)} %get-tuple-element.13.numerator_ref, f32[96,256]{1,0:T(8,128)S(1)} %get-tuple-element.14.denominator_ref), custom_call_target="tpu_custom_call" | custom-call | flops 122880 | bytes 688128 | tf_op jit(solution)/shard_map/pallas_call | solution.py:481
Async XLA Ops:
  0.6 38.2 %copy-start.2 = (f32[4,112,128]{2,1,0:T(8,128)S(1)}, f32[4,112,128]{2,1,0:T(8,128)}, u32[]{:S(2)}) copy-start(f32[4,112,128]{2,1,0:T(8,128)} %constant.17.clone.class_ref) | copy-start | bytes 688132
  0.6 38.2 %copy-start.4 = (bf16[384,224]{1,0:T(8,128)(2,1)S(1)}, bf16[384,224]{1,0:T(8,128)(2,1)}, u32[]{:S(2)}) copy-start(bf16[384,224]{1,0:T(8,128)(2,1)} %constant.16.clone.out_table) | copy-start | bytes 516100
  0.7 38.2 %copy-start = (bf16[512,256]{1,0:T(8,128)(2,1)S(1)}, bf16[512,256]{1,0:T(8,128)(2,1)}, u32[]{:S(2)}) copy-start(bf16[512,256]{1,0:T(8,128)(2,1)} %constant.15.clone.back_ref) | copy-start | bytes 786436
  0.7 38.2 %copy-start.1 = (bf16[512,256]{1,0:T(8,128)(2,1)S(1)}, bf16[512,256]{1,0:T(8,128)(2,1)}, u32[]{:S(2)}) copy-start(bf16[512,256]{1,0:T(8,128)(2,1)} %constant.14.clone.fine_ref) | copy-start | bytes 786436
  0.7 38.2 %copy-start.3 = (bf16[448,192]{1,0:T(8,128)(2,1)S(1)}, bf16[448,192]{1,0:T(8,128)(2,1)}, u32[]{:S(2)}) copy-start(bf16[448,192]{1,0:T(8,128)(2,1)} %constant.13.clone.coarse_ref) | copy-start | bytes 516100
  54.1 12.2 %all-to-all-start.3 = ((f32[8,96,128]{2,1,0:T(8,128)}), f32[8,96,128]{2,1,0:T(8,128)S(1)}, u32[]{:S(2)}, u32[]{:S(2)}) async-start(f32[8,96,128]{2,1,0:T(8,128)} %bitcast.5), calls=%async_computation.3 | async-start | bytes 786432 | tf_op jit(solution)/shard_map/all_to_all | solution.py:391

commit v5 on v4

--- a/solution.py
+++ b/solution.py
@@ -39,12 +39,13 @@
 SPEC_ROWS = 112
 
 ORDER = "hxzc"
+Z_FIRST = 5
 SIZES = {"h": 2, "x": 2, "z": 8, "c": 2}
 WEIGHTS = {name: math.prod(SIZES[k] for k in ORDER[at + 1 :]) for at, name in enumerate(ORDER)}
 DIGITS = [
     {name: place // WEIGHTS[name] % SIZES[name] for name in ORDER} for place in range(PAIR_SIZE)
 ]
-PIECES = [(16 * d["x"] + 2 * d["z"] + d["c"], d["h"]) for d in DIGITS]
+PIECES = [(16 * d["x"] + 2 * ((d["z"] + Z_FIRST) % 8) + d["c"], d["h"]) for d in DIGITS]
 
 F32 = jnp.float32
 BF16 = jnp.bfloat16
@@ -178,7 +179,7 @@
     place = (
         depth_pos % 2 * WEIGHTS["h"]
         + strike_pos // 16 * WEIGHTS["x"]
-        + strike_pos // 2 % 8 * WEIGHTS["z"]
+        + (strike_pos // 2 + 8 - Z_FIRST) % 8 * WEIGHTS["z"]
         + strike_pos % 2 * WEIGHTS["c"]
     )
     base = depth_pos // 2 * PAIR_MODES + place

time: 67.5 us -> 64.7 us (0.959)
  blocking collectives: 49.6 us -> 47.2 us
    all_to_all x2, blocking collectives: 33.7 us -> 31.3 us  [over_pair(): lax.all_to_all(pieces, ('depth', 'strike'), split_axis=0, concat_axis=0,...]
where the time goes in v5:
time: 64.7 us; the launch traced here: 64.4 us
  blocking collectives  47.2 us (73%)
  Pallas kernels  10.3 us (16%)
  starting transfers between devices  3.76 us (6%)
  waiting for transfers between devices  2.36 us (4%)
  between operations  0.73 us (1%)
    all_to_all x2, blocking collectives, over_pair(): lax.all_to_all(pieces, ('depth', 'strike'), split_axis=0, concat_axis=0,...  31.3 us
    all_to_all x1, blocking collectives, over_depth(): return lax.all_to_all(pieces, 'depth', split_axis=0, concat_axis=0)  15.9 us
    pallas_call x1, Pallas kernels, shards(): pl.pallas_call(stencil_kernel, out_shape=(shape(ROWS, COLS), pltpu.VMEM((...  5.88 us
    all_to_all x1, starting transfers between devices, over_depth(): return lax.all_to_all(pieces, 'depth', split_axis=0, concat_axis=0)  3.76 us
    all_to_all x1, waiting for transfers between devices, over_depth(): return lax.all_to_all(pieces, 'depth', split_axis=0, concat_axis=0)  2.36 us
  transfers between devices with their start and end apart: 1, of which 1 were waited for; matrix products, arithmetic and copies ran while one was open for 0% of the time, Pallas kernels for 9%

profile of v5, /device:TPU:1, one launch (start us, length us, event | category | flops | bytes accessed | tf_op | source)
XLA Modules:
  0.0 64.4 jit_solution(9239204825493273449)
XLA Ops:
  0.6 0.0 copy-start.2
  0.6 0.0 copy-start.4
  0.7 0.0 copy-start
  0.7 0.0 copy-start.1
  0.7 0.0 copy-start.3
  0.7 1.3 %shard_map.174 = (f32[8,96,128]{2,1,0:T(8,128)S(1)}, bf16[384,768]{1,0:T(8,128)(2,1)S(1)}) custom-call(f32[96,256]{1,0:T(8,128)} %speed_hbm.3, f32[96,256]{1,0:T(8,128)} %slip_hbm.1, bf16[4,384,768]{2,1,0:T(8,128)(2,1)} %constant.12.clone.table_hbm), custom_call_target="tpu_custom_call" | custom-call | flops 49152 | bytes 1179648 | tf_op jit(solution)/shard_map/pallas_call | solution.py:401
  2.0 15.9 %all_to_all.20 = f32[8,96,128]{2,1,0:T(8,128)S(1)} all-to-all(f32[8,96,128]{2,1,0:T(8,128)S(1)} %get-tuple-element.11), channel_id=1, replica_groups=mesh['strike'=32,'depth'=8] {'depth'}, dimensions={0} | all-to-all | bytes 786432 | tf_op jit(solution)/shard_map/all_to_all | solution.py:392
  17.9 0.4 shard_map.175
  18.3 18.2 %all_to_all.21 = f32[64,1,384]{2,1,0:T(1,128)S(1)} all-to-all(f32[64,1,384]{2,1,0:T(1,128)S(1)} %bitcast.8), channel_id=1, replica_groups={{80,88,96,104,112,120,0,8,16,24,32,40,48,56,64,72,208,216,224,232,240,2..., dimensions={0} | all-to-all | bytes 196608 | tf_op jit(solution)/shard_map/all_to_all | solution.py:396
  36.5 0.0 copy-done.2
  36.5 0.0 copy-done.4
  36.5 0.0 copy-done
  36.5 0.0 copy-done.1
  36.5 0.0 copy-done.3
  36.5 0.9 %shard_map.176 = f32[192,128]{1,0:T(8,128)S(1)} custom-call(f32[192,128]{1,0:T(8,128)S(1)} %bitcast.9, bf16[448,192]{1,0:T(8,128)(2,1)S(1)} %copy-done.3, bf16[512,256]{1,0:T(8,128)(2,1)S(1)} %copy-done.1, bf16[512,256]{1,0:T(8,128)(2,1)S(1)} %copy-done, bf16[384,224]{1,0:T(8,128)(2,1)S(1)} %copy-done.4, f32[4,112,128]{2,1,0:T(8,128)S(1)} %copy-done.2), custom_call_target="tpu_custom_call" | custom-call | flops 201326592 | bytes 1474560 | tf_op jit(solution)/shard_map/pallas_call | solution.py:425
  37.4 13.1 %all_to_all.22 = f32[64,1,384]{2,1,0:T(1,128)S(1)} all-to-all(f32[64,1,384]{2,1,0:T(1,128)S(1)} %bitcast.10), channel_id=1, replica_groups={{80,88,96,104,112,120,0,8,16,24,32,40,48,56,64,72,208,216,224,232,240,2..., dimensions={0} | all-to-all | bytes 196608 | tf_op jit(solution)/shard_map/all_to_all | solution.py:396
  50.5 1.2 %shard_map.177 = f32[768,128]{1,0:T(8,128)} custom-call(f32[192,128]{1,0:T(8,128)S(1)} %bitcast.7, bf16[384,768]{1,0:T(8,128)(2,1)S(1)} %get-tuple-element.12.table_ref), custom_call_target="tpu_custom_call" | custom-call | flops 113246208 | bytes 1179648 | tf_op jit(solution)/shard_map/pallas_call | solution.py:441
  51.7 3.8 %all-to-all-start.3 = ((f32[8,96,128]{2,1,0:T(8,128)}), f32[8,96,128]{2,1,0:T(8,128)S(1)}, u32[]{:S(2)}, u32[]{:S(2)}) async-start(f32[8,96,128]{2,1,0:T(8,128)} %bitcast.5), calls=%async_computation.3 | async-start | bytes 786432 | tf_op jit(solution)/shard_map/all_to_all | solution.py:392
  55.5 5.9 %shard_map.178 = (f32[96,256]{1,0:T(8,128)}, f32[96,256]{1,0:T(8,128)S(1)}, f32[96,256]{1,0:T(8,128)S(1)}, f32[32,96,256]{2,1,0:T(8,128)}, f32[32,96,256]{2,1,0:T(8,128)}) custom-call(f32[96,256]{1,0:T(8,128)} %speed_hbm.3, f32[96,256]{1,0:T(8,128)} %memory_hbm.1, f32[96,256]{1,0:T(8,128)} %clamping_hbm.1, f32[96,256]{1,0:T(8,128)} %effect_a_hbm.1, ...), custom_call_target="tpu_custom_call" | custom-call | flops 14155776 | bytes 13467648 | tf_op jit(solution)/shard_map/pallas_call | solution.py:452
  61.3 2.4 %all-to-all-done.3.parts_ref = f32[8,96,128]{2,1,0:T(8,128)S(1)} async-done(((f32[8,96,128]{2,1,0:T(8,128)}), f32[8,96,128]{2,1,0:T(8,128)S(1)}, u32[]{:S(2)}, u32[]{:S(2)}) %all-to-all-start.3) | async-done | bytes 393248 | tf_op jit(solution)/shard_map/all_to_all | solution.py:392
  63.7 0.7 %shard_map.179 = f32[96,256]{1,0:T(8,128)} custom-call(f32[8,96,128]{2,1,0:T(8,128)S(1)} %all-to-all-done.3.parts_ref, f32[96,256]{1,0:T(8,128)S(1)} %get-tuple-element.13.numerator_ref, f32[96,256]{1,0:T(8,128)S(1)} %get-tuple-element.14.denominator_ref), custom_call_target="tpu_custom_call" | custom-call | flops 122880 | bytes 688128 | tf_op jit(solution)/shard_map/pallas_call | solution.py:482
Async XLA Ops:
  0.6 35.8 %copy-start.2 = (f32[4,112,128]{2,1,0:T(8,128)S(1)}, f32[4,112,128]{2,1,0:T(8,128)}, u32[]{:S(2)}) copy-start(f32[4,112,128]{2,1,0:T(8,128)} %constant.17.clone.class_ref) | copy-start | bytes 688132
  0.6 35.8 %copy-start.4 = (bf16[384,224]{1,0:T(8,128)(2,1)S(1)}, bf16[384,224]{1,0:T(8,128)(2,1)}, u32[]{:S(2)}) copy-start(bf16[384,224]{1,0:T(8,128)(2,1)} %constant.16.clone.out_table) | copy-start | bytes 516100
  0.7 35.8 %copy-start = (bf16[512,256]{1,0:T(8,128)(2,1)S(1)}, bf16[512,256]{1,0:T(8,128)(2,1)}, u32[]{:S(2)}) copy-start(bf16[512,256]{1,0:T(8,128)(2,1)} %constant.15.clone.back_ref) | copy-start | bytes 786436
  0.7 35.8 %copy-start.1 = (bf16[512,256]{1,0:T(8,128)(2,1)S(1)}, bf16[512,256]{1,0:T(8,128)(2,1)}, u32[]{:S(2)}) copy-start(bf16[512,256]{1,0:T(8,128)(2,1)} %constant.14.clone.fine_ref) | copy-start | bytes 786436
  0.7 35.8 %copy-start.3 = (bf16[448,192]{1,0:T(8,128)(2,1)S(1)}, bf16[448,192]{1,0:T(8,128)(2,1)}, u32[]{:S(2)}) copy-start(bf16[448,192]{1,0:T(8,128)(2,1)} %constant.13.clone.coarse_ref) | copy-start | bytes 516100
  51.7 12.0 %all-to-all-start.3 = ((f32[8,96,128]{2,1,0:T(8,128)}), f32[8,96,128]{2,1,0:T(8,128)S(1)}, u32[]{:S(2)}, u32[]{:S(2)}) async-start(f32[8,96,128]{2,1,0:T(8,128)} %bitcast.5), calls=%async_computation.3 | async-start | bytes 786432 | tf_op jit(solution)/shard_map/all_to_all | solution.py:392

commit v6 on v5

--- a/solution.py
+++ b/solution.py
@@ -40,6 +40,7 @@
 
 ORDER = "hxzc"
 Z_FIRST = 5
+DEPTH_ORDER = [7, 4, 5, 6, 3, 0, 1, 2]
 SIZES = {"h": 2, "x": 2, "z": 8, "c": 2}
 WEIGHTS = {name: math.prod(SIZES[k] for k in ORDER[at + 1 :]) for at, name in enumerate(ORDER)}
 DIGITS = [
@@ -60,7 +61,8 @@
 def depth_table():
     index = np.arange(DEPTH)
     angle = 2.0 * np.pi / DEPTH * (index[:, None] * index[None, :] % DEPTH)
-    return np.cos(angle) + np.sin(angle)
+    table = (np.cos(angle) + np.sin(angle)).reshape(DEPTH, DEPTH_PARTS, ROWS)
+    return table[:, DEPTH_ORDER].reshape(DEPTH, DEPTH)
 
 
 def coarse_tables():
@@ -159,7 +161,7 @@
     loads[1].wait()
     field = speed_ref[...] + RELAXATION * slip_ref[...]
     for part in range(DEPTH_PARTS):
-        half = part % 2
+        half = DEPTH_ORDER[part] % 2
         out_ref[part] = field[:, half * LANES : (half + 1) * LANES]
     for load in loads[2:]:
         load.wait()
@@ -221,9 +223,10 @@
 def final_kernel(parts_ref, numerator_ref, denominator_ref, out_ref):
     for half in range(2):
         lanes = slice(half * LANES, (half + 1) * LANES)
-        filtered = (parts_ref[half] + parts_ref[half + 2]) + (
-            parts_ref[half + 4] + parts_ref[half + 6]
-        )
+        one, two, three, four = (
+            parts_ref[part] for part in range(DEPTH_PARTS) if DEPTH_ORDER[part] % 2 == half
+        )
+        filtered = (one + two) + (three + four)
         out_ref[:, lanes] = (filtered + numerator_ref[:, lanes]) / denominator_ref[:, lanes]
 
 
@@ -389,7 +392,9 @@
     ]
 
     def over_depth(pieces):
-        return lax.all_to_all(pieces, "depth", split_axis=0, concat_axis=0)
+        return lax.all_to_all(
+            pieces, "depth", split_axis=0, concat_axis=0, axis_index_groups=[DEPTH_ORDER]
+        )
 
     def over_pair(pieces):
         pieces = pieces.reshape(PAIR_SIZE, 1, MODES * LANES)

time: 64.7 us -> 64.3 us (level)
  starting transfers between devices: 3.76 us -> 8.21 us
  blocking collectives: 47.2 us -> 44.7 us
  waiting for transfers between devices: 2.36 us -> 0.01 us
    all_to_all x1, starting transfers between devices: 3.76 us -> 8.21 us  [over_depth(): lax.all_to_all(pieces, 'depth', split_axis=0, concat_axis=0, axis_index_g...]
    all_to_all x1, blocking collectives: 15.9 us -> 12.8 us  [over_depth(): lax.all_to_all(pieces, 'depth', split_axis=0, concat_axis=0, axis_index_g...]
    all_to_all x1, waiting for transfers between devices: 2.36 us -> 0.01 us  [over_depth(): lax.all_to_all(pieces, 'depth', split_axis=0, concat_axis=0, axis_index_g...]
  transfers between devices with their start and end apart: 1 -> 1, of which waited for: 1 -> 0; matrix products, arithmetic and copies ran while one was open for 0% -> 0% of each run, Pallas kernels for 9% -> 9%
where the time goes in v6:
time: 64.3 us; the launch traced here: 64 us
  blocking collectives  44.7 us (70%)
  Pallas kernels  10.3 us (16%)
  starting transfers between devices  8.21 us (13%)
  between operations  0.74 us (1%)
    all_to_all x2, blocking collectives, over_pair(): lax.all_to_all(pieces, ('depth', 'strike'), split_axis=0, concat_axis=0,...  31.8 us
    all_to_all x1, blocking collectives, over_depth(): lax.all_to_all(pieces, 'depth', split_axis=0, concat_axis=0, axis_index_g...  12.8 us
    all_to_all x1, starting transfers between devices, over_depth(): lax.all_to_all(pieces, 'depth', split_axis=0, concat_axis=0, axis_index_g...  8.21 us
    pallas_call x1, Pallas kernels, shards(): pl.pallas_call(stencil_kernel, out_shape=(shape(ROWS, COLS), pltpu.VMEM((...  5.88 us
  transfers between devices with their start and end apart: 1, of which 0 were waited for; matrix products, arithmetic and copies ran while one was open for 0% of the time, Pallas kernels for 9%

profile of v6, /device:TPU:1, one launch (start us, length us, event | category | flops | bytes accessed | tf_op | source)
XLA Modules:
  0.0 64.0 jit_solution(17677120698799010434)
XLA Ops:
  0.6 0.0 copy-start.2
  0.6 0.0 copy-start.4
  0.7 0.0 copy-start
  0.7 0.0 copy-start.1
  0.7 0.0 copy-start.3
  0.7 1.3 %shard_map.174 = (f32[8,96,128]{2,1,0:T(8,128)S(1)}, bf16[384,768]{1,0:T(8,128)(2,1)S(1)}) custom-call(f32[96,256]{1,0:T(8,128)} %speed_hbm.3, f32[96,256]{1,0:T(8,128)} %slip_hbm.1, bf16[4,384,768]{2,1,0:T(8,128)(2,1)} %constant.12.clone.table_hbm), custom_call_target="tpu_custom_call" | custom-call | flops 49152 | bytes 1179648 | tf_op jit(solution)/shard_map/pallas_call | solution.py:406
  2.0 12.8 %all_to_all.20 = f32[8,96,128]{2,1,0:T(8,128)S(1)} all-to-all(f32[8,96,128]{2,1,0:T(8,128)S(1)} %get-tuple-element.11), channel_id=1, replica_groups={{7,4,5,6,3,0,1,2},{15,12,13,14,11,8,9,10},{23,20,21,22,19,16,17,18},{31..., dimensions={0} | all-to-all | bytes 786432 | tf_op jit(solution)/shard_map/all_to_all | solution.py:395
  14.8 0.4 shard_map.175
  15.2 18.7 %all_to_all.21 = f32[64,1,384]{2,1,0:T(1,128)S(1)} all-to-all(f32[64,1,384]{2,1,0:T(1,128)S(1)} %bitcast.8), channel_id=1, replica_groups={{80,88,96,104,112,120,0,8,16,24,32,40,48,56,64,72,208,216,224,232,240,2..., dimensions={0} | all-to-all | bytes 196608 | tf_op jit(solution)/shard_map/all_to_all | solution.py:401
  34.0 0.0 copy-done.2
  34.0 0.0 copy-done.4
  34.0 0.0 copy-done
  34.0 0.0 copy-done.1
  34.0 0.0 copy-done.3
  34.0 0.9 %shard_map.176 = f32[192,128]{1,0:T(8,128)S(1)} custom-call(f32[192,128]{1,0:T(8,128)S(1)} %bitcast.9, bf16[448,192]{1,0:T(8,128)(2,1)S(1)} %copy-done.3, bf16[512,256]{1,0:T(8,128)(2,1)S(1)} %copy-done.1, bf16[512,256]{1,0:T(8,128)(2,1)S(1)} %copy-done, bf16[384,224]{1,0:T(8,128)(2,1)S(1)} %copy-done.4, f32[4,112,128]{2,1,0:T(8,128)S(1)} %copy-done.2), custom_call_target="tpu_custom_call" | custom-call | flops 201326592 | bytes 1474560 | tf_op jit(solution)/shard_map/pallas_call | solution.py:430
  34.9 13.1 %all_to_all.22 = f32[64,1,384]{2,1,0:T(1,128)S(1)} all-to-all(f32[64,1,384]{2,1,0:T(1,128)S(1)} %bitcast.10), channel_id=1, replica_groups={{80,88,96,104,112,120,0,8,16,24,32,40,48,56,64,72,208,216,224,232,240,2..., dimensions={0} | all-to-all | bytes 196608 | tf_op jit(solution)/shard_map/all_to_all | solution.py:401
  48.0 1.2 %shard_map.177 = f32[768,128]{1,0:T(8,128)} custom-call(f32[192,128]{1,0:T(8,128)S(1)} %bitcast.7, bf16[384,768]{1,0:T(8,128)(2,1)S(1)} %get-tuple-element.12.table_ref), custom_call_target="tpu_custom_call" | custom-call | flops 113246208 | bytes 1179648 | tf_op jit(solution)/shard_map/pallas_call | solution.py:446
  49.2 8.2 %all-to-all-start.3 = ((f32[8,96,128]{2,1,0:T(8,128)}), f32[8,96,128]{2,1,0:T(8,128)S(1)}, u32[]{:S(2)}, u32[]{:S(2)}) async-start(f32[8,96,128]{2,1,0:T(8,128)} %bitcast.5), calls=%async_computation.3 | async-start | bytes 786432 | tf_op jit(solution)/shard_map/all_to_all | solution.py:395
  57.4 5.9 %shard_map.178 = (f32[96,256]{1,0:T(8,128)}, f32[96,256]{1,0:T(8,128)S(1)}, f32[96,256]{1,0:T(8,128)S(1)}, f32[32,96,256]{2,1,0:T(8,128)}, f32[32,96,256]{2,1,0:T(8,128)}) custom-call(f32[96,256]{1,0:T(8,128)} %speed_hbm.3, f32[96,256]{1,0:T(8,128)} %memory_hbm.1, f32[96,256]{1,0:T(8,128)} %clamping_hbm.1, f32[96,256]{1,0:T(8,128)} %effect_a_hbm.1, ...), custom_call_target="tpu_custom_call" | custom-call | flops 14155776 | bytes 13467648 | tf_op jit(solution)/shard_map/pallas_call | solution.py:457
  63.3 0.0 all-to-all-done.3.parts_ref
  63.3 0.7 %shard_map.179 = f32[96,256]{1,0:T(8,128)} custom-call(f32[8,96,128]{2,1,0:T(8,128)S(1)} %all-to-all-done.3.parts_ref, f32[96,256]{1,0:T(8,128)S(1)} %get-tuple-element.13.numerator_ref, f32[96,256]{1,0:T(8,128)S(1)} %get-tuple-element.14.denominator_ref), custom_call_target="tpu_custom_call" | custom-call | flops 122880 | bytes 688128 | tf_op jit(solution)/shard_map/pallas_call | solution.py:487
Async XLA Ops:
  0.6 33.3 %copy-start.2 = (f32[4,112,128]{2,1,0:T(8,128)S(1)}, f32[4,112,128]{2,1,0:T(8,128)}, u32[]{:S(2)}) copy-start(f32[4,112,128]{2,1,0:T(8,128)} %constant.17.clone.class_ref) | copy-start | bytes 688132
  0.6 33.3 %copy-start.4 = (bf16[384,224]{1,0:T(8,128)(2,1)S(1)}, bf16[384,224]{1,0:T(8,128)(2,1)}, u32[]{:S(2)}) copy-start(bf16[384,224]{1,0:T(8,128)(2,1)} %constant.16.clone.out_table) | copy-start | bytes 516100
  0.7 33.3 %copy-start = (bf16[512,256]{1,0:T(8,128)(2,1)S(1)}, bf16[512,256]{1,0:T(8,128)(2,1)}, u32[]{:S(2)}) copy-start(bf16[512,256]{1,0:T(8,128)(2,1)} %constant.15.clone.back_ref) | copy-start | bytes 786436
  0.7 33.3 %copy-start.1 = (bf16[512,256]{1,0:T(8,128)(2,1)S(1)}, bf16[512,256]{1,0:T(8,128)(2,1)}, u32[]{:S(2)}) copy-start(bf16[512,256]{1,0:T(8,128)(2,1)} %constant.14.clone.fine_ref) | copy-start | bytes 786436
  0.7 33.3 %copy-start.3 = (bf16[448,192]{1,0:T(8,128)(2,1)S(1)}, bf16[448,192]{1,0:T(8,128)(2,1)}, u32[]{:S(2)}) copy-start(bf16[448,192]{1,0:T(8,128)(2,1)} %constant.13.clone.coarse_ref) | copy-start | bytes 516100
  49.2 14.1 %all-to-all-start.3 = ((f32[8,96,128]{2,1,0:T(8,128)}), f32[8,96,128]{2,1,0:T(8,128)S(1)}, u32[]{:S(2)}, u32[]{:S(2)}) async-start(f32[8,96,128]{2,1,0:T(8,128)} %bitcast.5), calls=%async_computation.3 | async-start | bytes 786432 | tf_op jit(solution)/shard_map/all_to_all | solution.py:395

commit v7 on v6

--- a/solution.py
+++ b/solution.py
@@ -40,7 +40,7 @@
 
 ORDER = "hxzc"
 Z_FIRST = 5
-DEPTH_ORDER = [7, 4, 5, 6, 3, 0, 1, 2]
+DEPTH_ORDER = [3, 0, 1, 2, 7, 4, 5, 6]
 SIZES = {"h": 2, "x": 2, "z": 8, "c": 2}
 WEIGHTS = {name: math.prod(SIZES[k] for k in ORDER[at + 1 :]) for at, name in enumerate(ORDER)}
 DIGITS = [

time: 64.3 us -> 64.4 us (level)
  starting transfers between devices: 8.21 us -> 5.31 us
  waiting for transfers between devices: 0.01 us -> 1.56 us
  blocking collectives: 44.7 us -> 46.1 us
    all_to_all x1, starting transfers between devices: 8.21 us -> 5.31 us  [over_depth(): lax.all_to_all(pieces, 'depth', split_axis=0, concat_axis=0, axis_index_g...]
    all_to_all x1, blocking collectives: 12.8 us -> 14.9 us  [over_depth(): lax.all_to_all(pieces, 'depth', split_axis=0, concat_axis=0, axis_index_g...]
    all_to_all x1, waiting for transfers between devices: 0.01 us -> 1.56 us  [over_depth(): lax.all_to_all(pieces, 'depth', split_axis=0, concat_axis=0, axis_index_g...]
    all_to_all x2, blocking collectives: 31.8 us -> 31.2 us  [over_pair(): lax.all_to_all(pieces, ('depth', 'strike'), split_axis=0, concat_axis=0,...]
  transfers between devices with their start and end apart: 1 -> 1, of which waited for: 0 -> 1; matrix products, arithmetic and copies ran while one was open for 0% -> 0% of each run, Pallas kernels for 9% -> 9%
where the time goes in v7:
time: 64.4 us; the launch traced here: 64.1 us
  blocking collectives  46.1 us (72%)
  Pallas kernels  10.3 us (16%)
  starting transfers between devices  5.31 us (8%)
  waiting for transfers between devices  1.56 us (2%)
  between operations  0.73 us (1%)
    all_to_all x2, blocking collectives, over_pair(): lax.all_to_all(pieces, ('depth', 'strike'), split_axis=0, concat_axis=0,...  31.2 us
    all_to_all x1, blocking collectives, over_depth(): lax.all_to_all(pieces, 'depth', split_axis=0, concat_axis=0, axis_index_g...  14.9 us
    pallas_call x1, Pallas kernels, shards(): pl.pallas_call(stencil_kernel, out_shape=(shape(ROWS, COLS), pltpu.VMEM((...  5.88 us
    all_to_all x1, starting transfers between devices, over_depth(): lax.all_to_all(pieces, 'depth', split_axis=0, concat_axis=0, axis_index_g...  5.31 us
    all_to_all x1, waiting for transfers between devices, over_depth(): lax.all_to_all(pieces, 'depth', split_axis=0, concat_axis=0, axis_index_g...  1.56 us
  transfers between devices with their start and end apart: 1, of which 1 were waited for; matrix products, arithmetic and copies ran while one was open for 0% of the time, Pallas kernels for 9%

profile of v7, /device:TPU:1, one launch (start us, length us, event | category | flops | bytes accessed | tf_op | source)
XLA Modules:
  0.0 64.1 jit_solution(7875515173768967512)
XLA Ops:
  0.6 0.0 copy-start.2
  0.6 0.0 copy-start.4
  0.7 0.0 copy-start
  0.7 0.0 copy-start.1
  0.7 0.0 copy-start.3
  0.7 1.3 %shard_map.174 = (f32[8,96,128]{2,1,0:T(8,128)S(1)}, bf16[384,768]{1,0:T(8,128)(2,1)S(1)}) custom-call(f32[96,256]{1,0:T(8,128)} %speed_hbm.3, f32[96,256]{1,0:T(8,128)} %slip_hbm.1, bf16[4,384,768]{2,1,0:T(8,128)(2,1)} %constant.12.clone.table_hbm), custom_call_target="tpu_custom_call" | custom-call | flops 49152 | bytes 1179648 | tf_op jit(solution)/shard_map/pallas_call | solution.py:406
  2.0 14.9 %all_to_all.20 = f32[8,96,128]{2,1,0:T(8,128)S(1)} all-to-all(f32[8,96,128]{2,1,0:T(8,128)S(1)} %get-tuple-element.11), channel_id=1, replica_groups={{3,0,1,2,7,4,5,6},{11,8,9,10,15,12,13,14},{19,16,17,18,23,20,21,22},{27..., dimensions={0} | all-to-all | bytes 786432 | tf_op jit(solution)/shard_map/all_to_all | solution.py:395
  16.9 0.4 shard_map.175
  17.3 18.1 %all_to_all.21 = f32[64,1,384]{2,1,0:T(1,128)S(1)} all-to-all(f32[64,1,384]{2,1,0:T(1,128)S(1)} %bitcast.8), channel_id=1, replica_groups={{80,88,96,104,112,120,0,8,16,24,32,40,48,56,64,72,208,216,224,232,240,2..., dimensions={0} | all-to-all | bytes 196608 | tf_op jit(solution)/shard_map/all_to_all | solution.py:401
  35.4 0.0 copy-done.2
  35.4 0.0 copy-done.4
  35.4 0.0 copy-done
  35.4 0.0 copy-done.1
  35.4 0.0 copy-done.3
  35.4 0.9 %shard_map.176 = f32[192,128]{1,0:T(8,128)S(1)} custom-call(f32[192,128]{1,0:T(8,128)S(1)} %bitcast.9, bf16[448,192]{1,0:T(8,128)(2,1)S(1)} %copy-done.3, bf16[512,256]{1,0:T(8,128)(2,1)S(1)} %copy-done.1, bf16[512,256]{1,0:T(8,128)(2,1)S(1)} %copy-done, bf16[384,224]{1,0:T(8,128)(2,1)S(1)} %copy-done.4, f32[4,112,128]{2,1,0:T(8,128)S(1)} %copy-done.2), custom_call_target="tpu_custom_call" | custom-call | flops 201326592 | bytes 1474560 | tf_op jit(solution)/shard_map/pallas_call | solution.py:430
  36.3 13.1 %all_to_all.22 = f32[64,1,384]{2,1,0:T(1,128)S(1)} all-to-all(f32[64,1,384]{2,1,0:T(1,128)S(1)} %bitcast.10), channel_id=1, replica_groups={{80,88,96,104,112,120,0,8,16,24,32,40,48,56,64,72,208,216,224,232,240,2..., dimensions={0} | all-to-all | bytes 196608 | tf_op jit(solution)/shard_map/all_to_all | solution.py:401
  49.4 1.2 %shard_map.177 = f32[768,128]{1,0:T(8,128)} custom-call(f32[192,128]{1,0:T(8,128)S(1)} %bitcast.7, bf16[384,768]{1,0:T(8,128)(2,1)S(1)} %get-tuple-element.12.table_ref), custom_call_target="tpu_custom_call" | custom-call | flops 113246208 | bytes 1179648 | tf_op jit(solution)/shard_map/pallas_call | solution.py:446
  50.6 5.3 %all-to-all-start.3 = ((f32[8,96,128]{2,1,0:T(8,128)}), f32[8,96,128]{2,1,0:T(8,128)S(1)}, u32[]{:S(2)}, u32[]{:S(2)}) async-start(f32[8,96,128]{2,1,0:T(8,128)} %bitcast.5), calls=%async_computation.3 | async-start | bytes 786432 | tf_op jit(solution)/shard_map/all_to_all | solution.py:395
  55.9 5.9 %shard_map.178 = (f32[96,256]{1,0:T(8,128)}, f32[96,256]{1,0:T(8,128)S(1)}, f32[96,256]{1,0:T(8,128)S(1)}, f32[32,96,256]{2,1,0:T(8,128)}, f32[32,96,256]{2,1,0:T(8,128)}) custom-call(f32[96,256]{1,0:T(8,128)} %speed_hbm.3, f32[96,256]{1,0:T(8,128)} %memory_hbm.1, f32[96,256]{1,0:T(8,128)} %clamping_hbm.1, f32[96,256]{1,0:T(8,128)} %effect_a_hbm.1, ...), custom_call_target="tpu_custom_call" | custom-call | flops 14155776 | bytes 13467648 | tf_op jit(solution)/shard_map/pallas_call | solution.py:457
  61.8 1.6 %all-to-all-done.3.parts_ref = f32[8,96,128]{2,1,0:T(8,128)S(1)} async-done(((f32[8,96,128]{2,1,0:T(8,128)}), f32[8,96,128]{2,1,0:T(8,128)S(1)}, u32[]{:S(2)}, u32[]{:S(2)}) %all-to-all-start.3) | async-done | bytes 393248 | tf_op jit(solution)/shard_map/all_to_all | solution.py:395
  63.4 0.7 %shard_map.179 = f32[96,256]{1,0:T(8,128)} custom-call(f32[8,96,128]{2,1,0:T(8,128)S(1)} %all-to-all-done.3.parts_ref, f32[96,256]{1,0:T(8,128)S(1)} %get-tuple-element.13.numerator_ref, f32[96,256]{1,0:T(8,128)S(1)} %get-tuple-element.14.denominator_ref), custom_call_target="tpu_custom_call" | custom-call | flops 122880 | bytes 688128 | tf_op jit(solution)/shard_map/pallas_call | solution.py:487
Async XLA Ops:
  0.6 34.8 %copy-start.2 = (f32[4,112,128]{2,1,0:T(8,128)S(1)}, f32[4,112,128]{2,1,0:T(8,128)}, u32[]{:S(2)}) copy-start(f32[4,112,128]{2,1,0:T(8,128)} %constant.17.clone.class_ref) | copy-start | bytes 688132
  0.6 34.8 %copy-start.4 = (bf16[384,224]{1,0:T(8,128)(2,1)S(1)}, bf16[384,224]{1,0:T(8,128)(2,1)}, u32[]{:S(2)}) copy-start(bf16[384,224]{1,0:T(8,128)(2,1)} %constant.16.clone.out_table) | copy-start | bytes 516100
  0.7 34.7 %copy-start = (bf16[512,256]{1,0:T(8,128)(2,1)S(1)}, bf16[512,256]{1,0:T(8,128)(2,1)}, u32[]{:S(2)}) copy-start(bf16[512,256]{1,0:T(8,128)(2,1)} %constant.15.clone.back_ref) | copy-start | bytes 786436
  0.7 34.7 %copy-start.1 = (bf16[512,256]{1,0:T(8,128)(2,1)S(1)}, bf16[512,256]{1,0:T(8,128)(2,1)}, u32[]{:S(2)}) copy-start(bf16[512,256]{1,0:T(8,128)(2,1)} %constant.14.clone.fine_ref) | copy-start | bytes 786436
  0.7 34.7 %copy-start.3 = (bf16[448,192]{1,0:T(8,128)(2,1)S(1)}, bf16[448,192]{1,0:T(8,128)(2,1)}, u32[]{:S(2)}) copy-start(bf16[448,192]{1,0:T(8,128)(2,1)} %constant.13.clone.coarse_ref) | copy-start | bytes 516100
  50.6 12.8 %all-to-all-start.3 = ((f32[8,96,128]{2,1,0:T(8,128)}), f32[8,96,128]{2,1,0:T(8,128)S(1)}, u32[]{:S(2)}, u32[]{:S(2)}) async-start(f32[8,96,128]{2,1,0:T(8,128)} %bitcast.5), calls=%async_computation.3 | async-start | bytes 786432 | tf_op jit(solution)/shard_map/all_to_all | solution.py:395
